TPU v7x, 256 devices: a whole 4x4x8 slice. The times are simulated.
256 devices in a mesh: real: 8 (over x_hi, y), strike: 32 (over x_lo, z, core).
Axes of the slice: x: 4 (x_hi: 2, x_lo: 2; x = x_hi * 2 + x_lo), y: 4, z: 8, core: 2. Of those that a mesh axis runs over, the one named last changes fastest.
Arguments:
- grades: bfloat16 [8, 32, 64, 32, 128], P('real', None, 'strike'), may hold values from -6 to 6
- cotangent: bfloat16 [8, 32, 64, 32, 128], P('real', None, 'strike'), may hold values from -6 to 6
- weight: bfloat16 [32, 864], P('real'), may hold values from -0.21875 to 0.21875
- bias: bfloat16 [32], P('real'), may hold values from -3 to 3
Outputs:
- activation: bfloat16 [8, 32, 64, 32, 128], P('real', None, 'strike')
- grad_input: bfloat16 [8, 32, 64, 32, 128], P('real', None, 'strike')
- grad_weight: float32 [32, 864], P('real')
- grad_bias: float32 [32], P('real')
All inputs are finite; a program needn't handle non-finite values.
Results may differ from a plain program's by a relative error of at most 0.0095.
Values may be sent and summed in bfloat16 or wider, within the bound.
A program may use at most 128 MiB of HBM per device.

v0:
```python
import jax
import jax.numpy as jnp
from jax import lax
from jax.sharding import PartitionSpec as P


def padded(value, sides, width):
    for axis, dim in sides:
        peers, length = (lax.axis_size(axis), value.shape[dim])
        up = [(i, (i + 1) % peers) for i in range(peers - 1)]
        down = [(j, i) for i, j in up]
        last = lax.slice_in_dim(value, length - width, length, axis=dim)
        leading = lax.slice_in_dim(value, 0, width, axis=dim)
        before = lax.ppermute(last, axis, up)
        after = lax.ppermute(leading, axis, down)
        value = jnp.concatenate([before, value, after], axis=dim)
    return value


def tap_list():
    listing = []
    for shift_x in (-1, 0, 1):
        for shift_y in (-1, 0, 1):
            for shift_z in (-1, 0, 1):
                listing.append(
                    (
                        shift_x,
                        shift_y,
                        shift_z,
                        9 * (shift_x + 1) + 3 * (shift_y + 1) + (shift_z + 1),
                    )
                )
    return listing


def transposed_stencil(padded_grad, kernel3, planes, rows, depth):
    total = jnp.zeros((kernel3.shape[2], planes, rows, depth), jnp.float32)
    for shift_x, shift_y, shift_z, column in tap_list():
        window = padded_grad[
            :,
            1 - shift_x : 1 - shift_x + planes,
            1 - shift_y : 1 - shift_y + rows,
            1 - shift_z : 1 - shift_z + depth,
        ]
        total = total + jnp.einsum(
            "oi,oxyz->ixyz", kernel3[:, column, :], window, preferred_element_type=jnp.float32
        )
    return total


def local(grades, cotangent, weight, bias):
    field = grades[0]
    cot = cotangent[0]
    in_chan, planes, rows, depth = field.shape
    whole_weight, whole_bias = (
        lax.all_gather(weight, "real", axis=0, tiled=True),
        lax.all_gather(bias, "real", axis=0, tiled=True),
    )
    out_chan = whole_weight.shape[0]
    kernel3 = whole_weight.reshape(out_chan, 27, in_chan)
    haloed = padded(field, (("strike", 1),), 1)
    padded_in = jnp.pad(haloed, ((0, 0), (0, 0), (1, 1), (1, 1)))
    total = jnp.zeros((out_chan, planes, rows, depth), jnp.float32)
    for shift_x, shift_y, shift_z, column in tap_list():
        window = padded_in[
            :,
            1 + shift_x : 1 + shift_x + planes,
            1 + shift_y : 1 + shift_y + rows,
            1 + shift_z : 1 + shift_z + depth,
        ]
        total = total + jnp.einsum(
            "oi,ixyz->oxyz", kernel3[:, column, :], window, preferred_element_type=jnp.float32
        )
    pre = total + whole_bias.astype(jnp.float32)[:, None, None, None]
    sig = jax.nn.sigmoid(pre)
    activation = (pre * sig).astype(jnp.bfloat16)
    dpre = (cot.astype(jnp.float32) * sig * (1.0 + pre * (1.0 - sig))).astype(jnp.bfloat16)
    grad_haloed = padded(dpre, (("strike", 1),), 1)
    padded_grad = jnp.pad(grad_haloed, ((0, 0), (0, 0), (1, 1), (1, 1)))
    grad_field = transposed_stencil(padded_grad, kernel3, planes, rows, depth)
    grad_input = grad_field.astype(jnp.bfloat16)
    columns = []
    for shift_x, shift_y, shift_z, column in tap_list():
        window = padded_in[
            :,
            1 + shift_x : 1 + shift_x + planes,
            1 + shift_y : 1 + shift_y + rows,
            1 + shift_z : 1 + shift_z + depth,
        ]
        columns.append(
            jnp.einsum("oxyz,ixyz->oi", dpre, window, preferred_element_type=jnp.float32)
        )
    local_weight = jnp.stack(columns, axis=1).reshape(out_chan, 27 * in_chan)
    local_bias = jnp.sum(dpre.astype(jnp.float32), axis=(1, 2, 3))
    summed = lax.psum((local_weight, local_bias), "strike")
    owned_weight, owned_bias = (
        lax.psum_scatter(summed[0], "real", scatter_dimension=0, tiled=True),
        lax.psum_scatter(summed[1], "real", scatter_dimension=0, tiled=True),
    )
    cells = lax.axis_size("real") * lax.axis_size("strike") * planes * rows * depth
    factor = 1.0 / cells**0.5
    return (activation[None], grad_input[None], owned_weight * factor, owned_bias * factor)


def solution(mesh):
    in_specs = (
        P("real", None, "strike", None, None),
        P("real", None, "strike", None, None),
        P("real", None),
        P("real"),
    )
    out_specs = (
        P("real", None, "strike", None, None),
        P("real", None, "strike", None, None),
        P("real", None),
        P("real"),
    )
    return jax.shard_map(local, mesh=mesh, in_specs=in_specs, out_specs=out_specs, check_vma=False)
```

profile of v0, /device:TPU:1, one launch (start us, length us, event | category | flops | bytes accessed | tf_op | source)
XLA Modules:
  0.0 310.6 jit_solution(5188992377177821428)
XLA Ops:
  7.2 1.4 copy.380
  8.7 4.9 %collective-permute-start = (bf16[32,1,32,128]{3,0,2,1:T(8,128)(2,1)S(1)}, bf16[32,1,32,128]{3,0,2,1:T(8,128)(2,1)S(1)}, u32[]{:S(2)}, u32[]{:S(2)}) collective-permute-start(bf16[32,1,32,128]{3,0,2,1:T(8,128)(2,1)S(1)} %get-tuple-element.23), channel_id=1, source_target_pairs={{0,1},{1,2},{2,3},{3,4},{4,5},{5,6},{6,7},{7,8},{8,9},{9,10},{10,1... | collective-permute-start | bytes 786440 | tf_op jit(solution)/shard_map/ppermute | solution.py:14
  13.7 1.9 collective-permute-start.1
  15.6 29.0 %all-gather = bf16[8,4,864]{2,1,0:T(4,128)(2,1)S(1)} all-gather(bf16[1,4,864]{2,1,0:T(4,128)(2,1)} %bitcast.644), channel_id=1, replica_groups=mesh['real'=8,'strike'=32] {'real'}, dimensions={0}, use_global_device_ids=true | all-gather | bytes 62208 | tf_op jit(solution)/shard_map/all_gather | solution.py:56
  45.5 0.6 fusion.205
  47.0 20.0 %all-reduce.2 = bf16[32]{0:T(256)(128)(2,1)S(1)} all-reduce(bf16[32]{0:T(256)(128)(2,1)S(1)} %dynamic-update-slice), channel_id=1, replica_groups=mesh['real'=8,'strike'=32] {'real'}, use_global_device_ids=true, to_apply=%add.2 | all-reduce | flops 32 | bytes 128
  67.0 0.5 convert_element_type.24
  68.1 0.4 fusion.193
  68.6 1.6 select_maximum_fusion.2
  77.9 1.3 fusion.53
  79.5 2.0 convert_reduce_fusion
  83.5 0.4 fusion.79
  84.1 0.4 fusion.77
  84.5 0.4 fusion.76
  85.1 0.4 fusion.74
  86.2 0.7 fusion.71
  87.5 0.4 fusion.68
  88.5 0.4 fusion.65
  89.8 0.4 fusion.61
  90.4 0.4 fusion.59
  91.5 0.8 reshape.18
  92.4 9.6 %collective-permute-start.3 = (bf16[32,1,32,128]{3,0,2,1:T(8,128)(2,1)S(1)}, bf16[32,1,32,128]{3,0,2,1:T(8,128)(2,1)S(1)}, u32[]{:S(2)}, u32[]{:S(2)}) collective-permute-start(bf16[32,1,32,128]{3,0,2,1:T(8,128)(2,1)S(1)} %get-tuple-element.22), channel_id=1, source_target_pairs={{1,0},{2,1},{3,2},{4,3},{5,4},{6,5},{7,6},{8,7},{9,8},{10,9},{11,1... | collective-permute-start | bytes 786440 | tf_op jit(solution)/shard_map/ppermute | solution.py:15
  102.0 6.0 %collective-permute-start.2 = (bf16[32,1,32,128]{3,0,2,1:T(8,128)(2,1)S(1)}, bf16[32,1,32,128]{3,0,2,1:T(8,128)(2,1)S(1)}, u32[]{:S(2)}, u32[]{:S(2)}) collective-permute-start(bf16[32,1,32,128]{3,0,2,1:T(8,128)(2,1)S(1)} %get-tuple-element.21), channel_id=1, source_target_pairs={{0,1},{1,2},{2,3},{3,4},{4,5},{5,6},{6,7},{7,8},{8,9},{9,10},{10,1... | collective-permute-start | bytes 786440 | tf_op jit(solution)/shard_map/ppermute | solution.py:14
  108.0 1.0 copy.155
  109.0 15.5 %all-reduce.4 = f32[32]{0:T(128)S(1)} all-reduce(f32[32]{0:T(128)S(1)} %copy-done.41), channel_id=3, replica_groups=mesh['real'=8,'strike'=32] {'real'}, use_global_device_ids=true, to_apply=%region_4.5.clone | all-reduce | flops 32 | bytes 256
  124.6 58.2 %all-reduce.8.cloned.1.call-done = f32[32,864]{1,0:T(8,128)} async-done(((f32[32,864]{1,0:T(8,128)}), f32[32,864]{1,0:T(8,128)}) %all-reduce.8.cloned.1.call-update) | async-done | bytes 110608
  182.8 0.8 constant_dynamic-slice_fusion
  183.5 105.5 %all-reduce.5 = (f32[4,864]{1,0:T(4,128)S(1)}, f32[4]{0:T(128)S(1)}) all-reduce(f32[4,864]{1,0:T(4,128)S(1)} %constant_dynamic-slice_fusion, f32[4]{0:T(128)S(1)} %dynamic-slice.4), channel_id=1, replica_groups=mesh['real'=8,'strike'=32] {'strike'}, use_global_device_ids=true, to_apply=%region_0.1 | all-reduce | flops 3460 | bytes 27680 | tf_op jit(solution)/shard_map/psum | solution.py:95
  289.1 0.5 broadcast_multiply_fusion.1
  289.6 0.6 broadcast_multiply_fusion
  290.2 1.4 select_maximum_fusion
  291.6 0.4 fusion.108
  292.4 0.4 fusion.112
  292.8 0.4 fusion.114
  293.6 0.4 fusion.118
  294.0 0.4 fusion.120
  294.8 0.4 fusion.124
  295.5 0.4 fusion.128
  295.9 0.4 convolution_bitcast_fusion.14
  296.3 0.4 convolution_bitcast_fusion.15
  297.1 0.4 convolution_bitcast_fusion.17
  297.8 0.4 convolution_bitcast_fusion.19
  298.2 0.4 convolution_bitcast_fusion.20
  298.9 0.4 fusion.103
  299.3 0.4 fusion.105
  300.4 1.0 fusion.51
  301.8 1.0 fusion.57
  302.8 1.0 copy.156
  (156 shorter events, 18.6 us)
Async XLA Ops:
  7.2 38.3 %copy-start.40 = (u32[256]{0:T(256)S(1)}, u32[256]{0:T(256)}, u32[]{:S(2)}) copy-start(u32[256]{0:T(256)} %constant.20) | copy-start | bytes 3076
  7.2 61.0 %copy-start = (bf16[1,32,2,32,128]{4,3,2,1,0:T(8,128)(2,1)S(1)}, bf16[1,32,2,32,128]{4,3,2,1,0:T(8,128)(2,1)}, u32[]{:S(2)}) copy-start(bf16[1,32,2,32,128]{4,3,2,1,0:T(8,128)(2,1)} %param.4) | copy-start | bytes 1572868
  7.2 39.5 %copy-start.43 = (bf16[4]{0:T(256)(128)(2,1)S(1)}, bf16[4]{0:T(256)(128)(2,1)}, u32[]{:S(2)}) copy-start(bf16[4]{0:T(256)(128)(2,1)} %param.7) | copy-start | bytes 28
  7.2 175.6 %all-reduce.8.cloned.1.call-start = ((), (), s32[]{:S(2)}) async-start(), calls=%async_computation | async-start | bytes 229376
  8.7 59.8 %collective-permute-start = (bf16[32,1,32,128]{3,0,2,1:T(8,128)(2,1)S(1)}, bf16[32,1,32,128]{3,0,2,1:T(8,128)(2,1)S(1)}, u32[]{:S(2)}, u32[]{:S(2)}) collective-permute-start(bf16[32,1,32,128]{3,0,2,1:T(8,128)(2,1)S(1)} %get-tuple-element.23), channel_id=1, source_target_pairs={{0,1},{1,2},{2,3},{3,4},{4,5},{5,6},{6,7},{7,8},{8,9},{9,10},{10,1... | collective-permute-start | bytes 786440 | tf_op jit(solution)/shard_map/ppermute | solution.py:14
  13.7 54.9 %collective-permute-start.1 = (bf16[32,1,32,128]{3,0,2,1:T(8,128)(2,1)S(1)}, bf16[32,1,32,128]{3,0,2,1:T(8,128)(2,1)S(1)}, u32[]{:S(2)}, u32[]{:S(2)}) collective-permute-start(bf16[32,1,32,128]{3,0,2,1:T(8,128)(2,1)S(1)} %get-tuple-element.24), channel_id=1, source_target_pairs={{1,0},{2,1},{3,2},{4,3},{5,4},{6,5},{7,6},{8,7},{9,8},{10,9},{11,1... | collective-permute-start | bytes 786440 | tf_op jit(solution)/shard_map/ppermute | solution.py:15
  45.2 25.0 %copy-start.38 = (bf16[32,1,32]{2,1,0:T(2,128)(2,1)}, bf16[32,1,32]{2,1,0:T(2,128)(2,1)S(1)}, u32[]{:S(2)}) copy-start(bf16[32,1,32]{2,1,0:T(2,128)(2,1)S(1)} %get-tuple-element.37) | copy-start | bytes 6148
  45.2 25.0 %copy-start.26 = (bf16[32,1,32]{2,1,0:T(2,128)(2,1)}, bf16[32,1,32]{2,1,0:T(2,128)(2,1)S(1)}, u32[]{:S(2)}) copy-start(bf16[32,1,32]{2,1,0:T(2,128)(2,1)S(1)} %get-tuple-element.38) | copy-start | bytes 6148
  45.2 25.3 %copy-start.24 = (bf16[32,1,32]{2,1,0:T(2,128)(2,1)}, bf16[32,1,32]{2,1,0:T(2,128)(2,1)S(1)}, u32[]{:S(2)}) copy-start(bf16[32,1,32]{2,1,0:T(2,128)(2,1)S(1)} %get-tuple-element.39) | copy-start | bytes 6148
  45.2 25.7 %copy-start.22 = (bf16[32,1,32]{2,1,0:T(2,128)(2,1)}, bf16[32,1,32]{2,1,0:T(2,128)(2,1)S(1)}, u32[]{:S(2)}) copy-start(bf16[32,1,32]{2,1,0:T(2,128)(2,1)S(1)} %get-tuple-element.40) | copy-start | bytes 6148
  45.2 26.0 %copy-start.20 = (bf16[32,1,32]{2,1,0:T(2,128)(2,1)}, bf16[32,1,32]{2,1,0:T(2,128)(2,1)S(1)}, u32[]{:S(2)}) copy-start(bf16[32,1,32]{2,1,0:T(2,128)(2,1)S(1)} %get-tuple-element.41) | copy-start | bytes 6148
  45.2 26.3 %copy-start.18 = (bf16[32,1,32]{2,1,0:T(2,128)(2,1)}, bf16[32,1,32]{2,1,0:T(2,128)(2,1)S(1)}, u32[]{:S(2)}) copy-start(bf16[32,1,32]{2,1,0:T(2,128)(2,1)S(1)} %get-tuple-element.42) | copy-start | bytes 6148
  45.2 26.7 %copy-start.16 = (bf16[32,1,32]{2,1,0:T(2,128)(2,1)}, bf16[32,1,32]{2,1,0:T(2,128)(2,1)S(1)}, u32[]{:S(2)}) copy-start(bf16[32,1,32]{2,1,0:T(2,128)(2,1)S(1)} %get-tuple-element.43) | copy-start | bytes 6148
  45.2 28.7 %copy-start.14 = (bf16[32,1,32]{2,1,0:T(2,128)(2,1)}, bf16[32,1,32]{2,1,0:T(2,128)(2,1)S(1)}, u32[]{:S(2)}) copy-start(bf16[32,1,32]{2,1,0:T(2,128)(2,1)S(1)} %get-tuple-element.26) | copy-start | bytes 6148
  45.2 29.7 %copy-start.12 = (bf16[32,1,32]{2,1,0:T(2,128)(2,1)}, bf16[32,1,32]{2,1,0:T(2,128)(2,1)S(1)}, u32[]{:S(2)}) copy-start(bf16[32,1,32]{2,1,0:T(2,128)(2,1)S(1)} %get-tuple-element.27) | copy-start | bytes 6148
  45.3 30.0 %copy-start.8 = (bf16[32,1,32]{2,1,0:T(2,128)(2,1)}, bf16[32,1,32]{2,1,0:T(2,128)(2,1)S(1)}, u32[]{:S(2)}) copy-start(bf16[32,1,32]{2,1,0:T(2,128)(2,1)S(1)} %get-tuple-element.28) | copy-start | bytes 6148
  45.3 30.3 %copy-start.4 = (bf16[32,1,32]{2,1,0:T(2,128)(2,1)}, bf16[32,1,32]{2,1,0:T(2,128)(2,1)S(1)}, u32[]{:S(2)}) copy-start(bf16[32,1,32]{2,1,0:T(2,128)(2,1)S(1)} %get-tuple-element.30) | copy-start | bytes 6148
  45.4 26.9 %copy-start.36 = (bf16[32,1,32]{2,1,0:T(2,128)(2,1)}, bf16[32,1,32]{2,1,0:T(2,128)(2,1)S(1)}, u32[]{:S(2)}) copy-start(bf16[32,1,32]{2,1,0:T(2,128)(2,1)S(1)} %get-tuple-element.45) | copy-start | bytes 6148
  45.4 27.1 %copy-start.34 = (bf16[32,1,32]{2,1,0:T(2,128)(2,1)}, bf16[32,1,32]{2,1,0:T(2,128)(2,1)S(1)}, u32[]{:S(2)}) copy-start(bf16[32,1,32]{2,1,0:T(2,128)(2,1)S(1)} %get-tuple-element.46) | copy-start | bytes 6148
  45.4 27.5 %copy-start.32 = (bf16[32,1,32]{2,1,0:T(2,128)(2,1)}, bf16[32,1,32]{2,1,0:T(2,128)(2,1)S(1)}, u32[]{:S(2)}) copy-start(bf16[32,1,32]{2,1,0:T(2,128)(2,1)S(1)} %get-tuple-element.48) | copy-start | bytes 6148
  45.4 27.8 %copy-start.30 = (bf16[32,1,32]{2,1,0:T(2,128)(2,1)}, bf16[32,1,32]{2,1,0:T(2,128)(2,1)S(1)}, u32[]{:S(2)}) copy-start(bf16[32,1,32]{2,1,0:T(2,128)(2,1)S(1)} %get-tuple-element.49) | copy-start | bytes 6148
  45.4 28.1 %copy-start.28 = (bf16[32,1,32]{2,1,0:T(2,128)(2,1)}, bf16[32,1,32]{2,1,0:T(2,128)(2,1)S(1)}, u32[]{:S(2)}) copy-start(bf16[32,1,32]{2,1,0:T(2,128)(2,1)S(1)} %get-tuple-element.50) | copy-start | bytes 6148
  45.4 31.8 %copy-start.10 = (bf16[32,1,32]{2,1,0:T(2,128)(2,1)}, bf16[32,1,32]{2,1,0:T(2,128)(2,1)S(1)}, u32[]{:S(2)}) copy-start(bf16[32,1,32]{2,1,0:T(2,128)(2,1)S(1)} %get-tuple-element.51) | copy-start | bytes 6148
  45.5 32.2 %copy-start.6 = (bf16[32,1,32]{2,1,0:T(2,128)(2,1)}, bf16[32,1,32]{2,1,0:T(2,128)(2,1)S(1)}, u32[]{:S(2)}) copy-start(bf16[32,1,32]{2,1,0:T(2,128)(2,1)S(1)} %get-tuple-element.47) | copy-start | bytes 6148
  68.6 9.1 %copy-start.1 = (bf16[32,1,32,128]{3,0,2,1:T(8,128)(2,1)}, bf16[32,1,32,128]{3,0,2,1:T(8,128)(2,1)S(1)}, u32[]{:S(2)}) copy-start(bf16[32,1,32,128]{3,0,2,1:T(8,128)(2,1)S(1)} %collective-permute-done) | copy-start | bytes 786436
  77.9 1.6 copy-start.3
  77.9 1.6 copy-start.42
  79.5 2.3 copy-start.39
  81.8 1.4 copy-start.2
  90.8 18.2 %copy-start.41 = (f32[32]{0:T(128)S(1)}, f32[32]{0:T(128)}, u32[]{:S(2)}) copy-start(f32[32]{0:T(128)} %get-tuple-element.18) | copy-start | bytes 388
  92.4 199.2 %copy-start.27 = (bf16[32,1,32]{2,1,0:T(2,128)(2,1)S(1)}, bf16[32,1,32]{2,1,0:T(2,128)(2,1)}, u32[]{:S(2)}) copy-start(bf16[32,1,32]{2,1,0:T(2,128)(2,1)} %copy-done.26) | copy-start | bytes 6148
  92.4 197.8 %collective-permute-start.3 = (bf16[32,1,32,128]{3,0,2,1:T(8,128)(2,1)S(1)}, bf16[32,1,32,128]{3,0,2,1:T(8,128)(2,1)S(1)}, u32[]{:S(2)}, u32[]{:S(2)}) collective-permute-start(bf16[32,1,32,128]{3,0,2,1:T(8,128)(2,1)S(1)} %get-tuple-element.22), channel_id=1, source_target_pairs={{1,0},{2,1},{3,2},{4,3},{5,4},{6,5},{7,6},{8,7},{9,8},{10,9},{11,1... | collective-permute-start | bytes 786440 | tf_op jit(solution)/shard_map/ppermute | solution.py:15
  102.0 188.2 %collective-permute-start.2 = (bf16[32,1,32,128]{3,0,2,1:T(8,128)(2,1)S(1)}, bf16[32,1,32,128]{3,0,2,1:T(8,128)(2,1)S(1)}, u32[]{:S(2)}, u32[]{:S(2)}) collective-permute-start(bf16[32,1,32,128]{3,0,2,1:T(8,128)(2,1)S(1)} %get-tuple-element.21), channel_id=1, source_target_pairs={{0,1},{1,2},{2,3},{3,4},{4,5},{5,6},{6,7},{7,8},{8,9},{9,10},{10,1... | collective-permute-start | bytes 786440 | tf_op jit(solution)/shard_map/ppermute | solution.py:14
  290.2 1.8 copy-start.25
  291.6 1.2 copy-start.21
  292.0 1.2 copy-start.19
  292.4 1.2 copy-start.17
  292.8 1.2 copy-start.37
  293.2 1.2 copy-start.35
  293.6 1.2 copy-start.33
  294.0 1.2 copy-start.31
  294.4 1.1 copy-start.29
  294.8 1.2 copy-start.15
  295.2 1.2 copy-start.13
  295.5 1.2 copy-start.9
  295.9 1.1 copy-start.5
  298.6 1.1 copy-start.11
  298.9 1.1 copy-start.7
  (1 other events, 0.8 us)
Sparse Core Ops, SparseCore 0:
  92.5 90.2 all-reduce.7
where the time goes:
time: 315 us; the launch traced here: 311 us
  blocking collectives  170 us (54%)
  waiting for transfers between devices  58.3 us (19%)
  matrix products  31.7 us (10%)
  starting transfers between devices  22.5 us (7%)
  between operations  16.4 us (5%)
  local copies, waits for them, and re-layouts  7.13 us (2%)
  other arithmetic  4.62 us (1%)
    psum x1, blocking collectives, local(): summed = lax.psum((local_weight, local_bias), 'strike')  106 us
    unnamed x2, waiting for transfers between devices  58.2 us
    unnamed x2, blocking collectives  35.5 us
    all_gather x1, blocking collectives, local(): lax.all_gather(weight, 'real', axis=0, tiled=True)  29 us
    ppermute x2, starting transfers between devices, padded(): after = lax.ppermute(leading, axis, down)  11.5 us
    dot_general x27, matrix products, local(): jnp.einsum('oi,ixyz->oxyz', kernel3[:, column, :], window, preferred_elem...  11.4 us
    dot_general x27, matrix products, transposed_stencil(): jnp.einsum('oi,oxyz->ixyz', kernel3[:, column, :], window, preferred_elem...  11.1 us
    ppermute x2, starting transfers between devices, padded(): before = lax.ppermute(last, axis, up)  10.9 us
  transfers between devices with their start and end apart: 5, of which 1 were waited for; matrix products, arithmetic and copies ran while one was open for 2% of the time, Pallas kernels for 0%

commit v1 on v0

v1 whole, which is shorter than its diff:
```python
import functools

import jax
import jax.numpy as jnp
from jax import lax
from jax.experimental import pallas as pl
from jax.experimental.pallas import tpu as pltpu
from jax.sharding import PartitionSpec as P

MESH = pl.DeviceIdType.MESH
F32 = jnp.float32
BF16 = jnp.bfloat16
CH = 32
NY = 32
NZ = 128
WIDE = 4


def transpose_in(plane, work, put):
    def spread(c, carry):
        work[pl.ds(pl.multiple_of(c * NY, NY), NY), :] = plane(c).astype(F32)
        return carry

    lax.fori_loop(0, CH, spread, 0, unroll=8)

    def gather(y, carry):
        put(y, work[pl.ds(y, CH, NY), :])
        return carry

    lax.fori_loop(0, NY, gather, 0, unroll=8)


def stencil(buf, weights, x, y0):
    pieces = []
    for a in range(3):
        for b in range(3):
            pieces.append(jnp.concatenate([buf[x + a, y0 + j + b] for j in range(WIDE)], axis=1))
    cells = jnp.concatenate(pieces, axis=0)
    product = jnp.dot(weights[...], cells, preferred_element_type=F32)
    lane = lax.broadcasted_iota(jnp.int32, (CH, NZ), 1)
    out = []
    for j in range(WIDE):
        part = product[:, j * NZ : (j + 1) * NZ]
        low = pltpu.roll(part[0:CH], 1, 1)
        high = pltpu.roll(part[2 * CH : 3 * CH], NZ - 1, 1)
        out.append(
            part[CH : 2 * CH]
            + jnp.where(lane == 0, 0.0, low)
            + jnp.where(lane == NZ - 1, 0.0, high)
        )
    return out


def wait_for(ref, sem):
    pltpu.make_async_copy(ref, ref, sem).wait()


def kernel(
    real, xl, zs, co, planes, factor,
    grades, cot, wslot,
    act_out, gin_out, sum_out,
    gv, cv, work, field, dgrad, dshift, wf, wb, bias_col, slots, acc, bias_acc,
    send1, recv1, recv2, piece, act_v, gin_v,
    in_sem, w_send, w_recv, fs, fr, ds, dr, s1, r1, s2, r2, own_sem, out_sem,
):
    strike = xl * zs * co
    quarter = xl * co
    members = real * quarter
    per = CH // members
    me_r, me_s = lax.axis_index("real"), lax.axis_index("strike")
    my_x, my_z, my_c = me_s // (zs * co), lax.rem(me_s // co, zs), lax.rem(me_s, co)
    me_m = me_r * quarter + my_x * co + my_c

    def member(m):
        q = lax.rem(m, quarter)
        return m // quarter, (q // co) * (zs * co) + my_z * co + lax.rem(q, co)

    load_g = pltpu.make_async_copy(grades.at[0], gv, in_sem.at[0])
    load_c = pltpu.make_async_copy(cot.at[0], cv, in_sem.at[1])
    load_g.start()
    load_c.start()

    barrier = pltpu.get_barrier_semaphore()

    def greet_plane(k, carry):
        pl.semaphore_signal(
            barrier, inc=1, device_id=member(lax.rem(me_m + k, members)), device_id_type=MESH
        )
        return carry

    def greet_strike(k, carry):
        pl.semaphore_signal(
            barrier, inc=1, device_id=(me_r, lax.rem(me_s + k, strike)), device_id_type=MESH
        )
        return carry

    lax.fori_loop(1, members, greet_plane, 0)
    lax.fori_loop(1, strike, greet_strike, 0)

    zero = jnp.zeros((CH, NZ), BF16)
    for x in range(planes + 2):
        for buf in (field, dgrad):
            buf[x, 0] = zero
            buf[x, NY + 1] = zero

    def clear(buf, x):
        def row(y, carry):
            buf[x, y + 1] = zero
            return carry

        lax.fori_loop(0, NY, row, 0, unroll=8)

    @pl.when(me_s == 0)
    def _():
        clear(field, 0)
        clear(dgrad, 0)

    @pl.when(me_s == strike - 1)
    def _():
        clear(field, planes + 1)
        clear(dgrad, planes + 1)

    slots[me_r] = wslot[...]
    load_g.wait()
    for x in range(planes):

        def put(y, value, x=x):
            field[x + 1, y + 1] = value.astype(BF16)

        transpose_in(lambda c, x=x: gv[c, x], work, put)

    pl.semaphore_wait(barrier, members - 1 + strike - 1)

    def send_weight(k, carry):
        pltpu.make_async_remote_copy(
            src_ref=wslot,
            dst_ref=slots.at[me_r],
            send_sem=w_send,
            recv_sem=w_recv,
            device_id=(lax.rem(me_r + k, real), me_s),
            device_id_type=MESH,
        ).start()
        return carry

    lax.fori_loop(1, real, send_weight, 0)

    def halo(buf, send, recv, up):
        here, there = (planes, 0) if up else (1, planes + 1)
        i = 0 if up else 1
        return pltpu.make_async_remote_copy(
            src_ref=buf.at[here, pl.ds(1, NY)],
            dst_ref=buf.at[there, pl.ds(1, NY)],
            send_sem=send.at[i],
            recv_sem=recv.at[i],
            device_id=(me_r, me_s + 1 if up else me_s - 1),
            device_id_type=MESH,
        )

    def send_halo(buf, send, recv):
        @pl.when(me_s < strike - 1)
        def _():
            halo(buf, send, recv, True).start()

        @pl.when(me_s > 0)
        def _():
            halo(buf, send, recv, False).start()

    def sent_halo(buf, send):
        @pl.when(me_s < strike - 1)
        def _():
            wait_for(buf.at[planes, pl.ds(1, NY)], send.at[0])

        @pl.when(me_s > 0)
        def _():
            wait_for(buf.at[1, pl.ds(1, NY)], send.at[1])

    def got_halo(buf, recv):
        @pl.when(me_s > 0)
        def _():
            wait_for(buf.at[0, pl.ds(1, NY)], recv.at[0])

        @pl.when(me_s < strike - 1)
        def _():
            wait_for(buf.at[planes + 1, pl.ds(1, NY)], recv.at[1])

    send_halo(field, fs, fr)

    wait_for(slots.at[pl.ds(0, real - 1)], w_recv)
    gathered = slots[...].reshape(128, 256)
    row = lax.broadcasted_iota(jnp.int32, (128, 128), 0)
    col = lax.broadcasted_iota(jnp.int32, (128, 128), 1)
    order = (col == lax.rem(row, CH) * 4 + row // CH).astype(BF16)
    whole = jnp.dot(order, gathered, preferred_element_type=F32)
    turned = jnp.concatenate([whole[:, :128].T, whole[:, 128:].T], axis=0)
    for c in range(3):
        ahead, back = [], []
        for ab in range(9):
            t = 3 * ab + c
            ahead.append(whole[(t // 8) * CH : (t // 8 + 1) * CH, (t % 8) * CH : (t % 8 + 1) * CH])
            t = 26 - t
            back.append(turned[(t % 8) * CH : (t % 8 + 1) * CH, (t // 8) * CH : (t // 8 + 1) * CH])
        wf[pl.ds(c * CH, CH), :] = jnp.concatenate(ahead, axis=1).astype(BF16)
        wb[pl.ds(c * CH, CH), :] = jnp.concatenate(back, axis=1).astype(BF16)
    bias_col[...] = jnp.broadcast_to(whole[96:128, 96:97], (CH, NZ))

    load_c.wait()
    bias_acc[...] = jnp.zeros_like(bias_acc)
    got_halo(field, fr)
    lane = lax.broadcasted_iota(jnp.int32, (CH, NZ), 1)
    for x in range(planes):

        def spread(c, carry, x=x):
            work[pl.ds(pl.multiple_of(c * NY, NY), NY), :] = cv[c, x].astype(F32)
            return carry

        lax.fori_loop(0, CH, spread, 0, unroll=8)

        def forward(step, carry, x=x):
            y0 = step * WIDE
            for j, value in enumerate(stencil(field, wf, x, y0)):
                pre = value + bias_col[...]
                sig = jax.nn.sigmoid(pre)
                gin_v[pl.ds(y0 + j, CH, NY), :] = pre * sig
                upstream = work[pl.ds(y0 + j, CH, NY), :]
                dpre = (upstream * sig * (1.0 + pre * (1.0 - sig))).astype(BF16)
                dgrad[x + 1, y0 + j + 1] = dpre
                wide = dpre.astype(F32)
                bias_acc[...] += wide
                before = jnp.where(lane == NZ - 1, 0.0, pltpu.roll(wide, NZ - 1, 1))
                after = jnp.where(lane == 0, 0.0, pltpu.roll(wide, 1, 1))
                dshift[x, y0 + j] = jnp.concatenate(
                    [before.astype(BF16), dpre, after.astype(BF16)], axis=0
                )
            return carry

        lax.fori_loop(0, NY // WIDE, forward, 0)

        def pack(c, carry, x=x):
            act_v[c, x] = gin_v[pl.ds(pl.multiple_of(c * NY, NY), NY), :].astype(BF16)
            return carry

        lax.fori_loop(0, CH, pack, 0, unroll=8)

    send_halo(dgrad, ds, dr)
    store_act = pltpu.make_async_copy(act_v, act_out.at[0], out_sem.at[0])
    store_act.start()

    acc[...] = jnp.zeros_like(acc)
    for x in range(planes):

        def gram(step, carry, x=x):
            y0 = step * WIDE
            left = jnp.concatenate([dshift[x, y0 + j] for j in range(WIDE)], axis=1)
            pieces = []
            for a in range(3):
                for b in range(3):
                    pieces.append(
                        jnp.concatenate([field[x + a, y0 + j + b] for j in range(WIDE)], axis=1)
                    )
            right = jnp.concatenate(pieces, axis=0)
            acc[...] += lax.dot_general(
                left, right, (((1,), (1,)), ((), ())), preferred_element_type=F32
            )
            return carry

        lax.fori_loop(0, NY // WIDE, gram, 0)

    total = acc[...]
    tails = []
    for c in range(3):
        block = total[c * CH : (c + 1) * CH]
        send1[pl.ds(2 * c, CH, 8), :] = block[:, 0:128]
        send1[pl.ds(2 * c + 1, CH, 8), :] = block[:, 128:256]
        tails.append(block[:, 256:288])
    send1[pl.ds(6, CH, 8), :] = jnp.concatenate(tails + [jnp.zeros((CH, 32), F32)], axis=1)
    send1[pl.ds(7, CH, 8), :] = bias_acc[...]

    rows = per * 8

    def chunk(m):
        return send1.at[pl.ds(pl.multiple_of(m * rows, 8), rows)]

    def scatter(k, carry):
        m = lax.rem(me_m + k, members)
        pltpu.make_async_remote_copy(
            src_ref=chunk(m),
            dst_ref=recv1.at[me_m],
            send_sem=s1,
            recv_sem=r1,
            device_id=member(m),
            device_id_type=MESH,
        ).start()
        return carry

    lax.fori_loop(1, members, scatter, 0)
    own = pltpu.make_async_copy(chunk(me_m), recv1.at[me_m], own_sem)
    own.start()

    def turn_out(x, y, value):
        gin_v[pl.ds(y, CH, NY), :] = value

    got_halo(dgrad, dr)

    def backward(x):
        def step_of(step, carry):
            y0 = step * WIDE
            for j, value in enumerate(stencil(dgrad, wb, x, y0)):
                gin_v[pl.ds(y0 + j, CH, NY), :] = value
            return carry

        lax.fori_loop(0, NY // WIDE, step_of, 0)

        def pack(c, carry):
            gv[c, x] = gin_v[pl.ds(pl.multiple_of(c * NY, NY), NY), :].astype(BF16)
            return carry

        lax.fori_loop(0, CH, pack, 0, unroll=8)

    backward(0)

    own.wait()
    wait_for(recv1.at[pl.ds(0, members - 1)], r1)
    plane_sum = recv1[0]
    for m in range(1, members):
        plane_sum = plane_sum + recv1[m]
    piece[...] = plane_sum
    recv2[me_s] = plane_sum

    def spread_sum(k, carry):
        pltpu.make_async_remote_copy(
            src_ref=piece,
            dst_ref=recv2.at[me_s],
            send_sem=s2,
            recv_sem=r2,
            device_id=(me_r, lax.rem(me_s + k, strike)),
            device_id_type=MESH,
        ).start()
        return carry

    lax.fori_loop(1, strike, spread_sum, 0)

    for x in range(1, planes):
        backward(x)
    store_gin = pltpu.make_async_copy(gv, gin_out.at[0], out_sem.at[1])
    store_gin.start()

    wait_for(recv2.at[pl.ds(0, strike - 1)], r2)
    for xi in range(xl):
        for ci in range(co):
            value = recv2[xi * zs * co + ci]
            for z in range(1, zs):
                value = value + recv2[(xi * zs + z) * co + ci]
            sum_out[xi * co + ci] = value * factor

    wait_for(slots.at[pl.ds(0, real - 1)], w_send)
    sent_halo(field, fs)
    sent_halo(dgrad, ds)
    wait_for(recv1.at[pl.ds(0, members - 1)], s1)
    wait_for(recv2.at[pl.ds(0, strike - 1)], s2)
    store_act.wait()
    store_gin.wait()


def local(grades, cotangent, weight, bias, *, real, xl, zs, co):
    planes = grades.shape[2]
    strike = xl * zs * co
    members = real * xl * co
    per = CH // members
    rows = weight.shape[0]
    cells = real * strike * planes * NY * NZ
    factor = 1.0 / cells**0.5
    wslot = jnp.concatenate(
        [weight, bias[:, None], jnp.zeros((rows, 1024 - 865), BF16)], axis=1
    ).reshape(rows * 4, 256)
    hbm = pl.BlockSpec(memory_space=pl.ANY)
    vmem = pl.BlockSpec(memory_space=pltpu.VMEM)
    block = (1, CH, planes, NY, NZ)
    act, gin, total = pl.pallas_call(
        functools.partial(kernel, real, xl, zs, co, planes, factor),
        out_shape=(
            jax.ShapeDtypeStruct(block, BF16),
            jax.ShapeDtypeStruct(block, BF16),
            jax.ShapeDtypeStruct((xl * co, per * 8, 128), F32),
        ),
        in_specs=[hbm, hbm, vmem],
        out_specs=(hbm, hbm, vmem),
        scratch_shapes=[
            pltpu.VMEM((CH, planes, NY, NZ), BF16),
            pltpu.VMEM((CH, planes, NY, NZ), BF16),
            pltpu.VMEM((CH * NY, NZ), F32),
            pltpu.VMEM((planes + 2, NY + 2, CH, NZ), BF16),
            pltpu.VMEM((planes + 2, NY + 2, CH, NZ), BF16),
            pltpu.VMEM((planes, NY, 3 * CH, NZ), BF16),
            pltpu.VMEM((3 * CH, 9 * CH), BF16),
            pltpu.VMEM((3 * CH, 9 * CH), BF16),
            pltpu.VMEM((CH, NZ), F32),
            pltpu.VMEM((real, rows * 4, 256), BF16),
            pltpu.VMEM((3 * CH, 9 * CH), F32),
            pltpu.VMEM((CH, NZ), F32),
            pltpu.VMEM((CH * 8, 128), F32),
            pltpu.VMEM((members, per * 8, 128), F32),
            pltpu.VMEM((strike, per * 8, 128), F32),
            pltpu.VMEM((per * 8, 128), F32),
            pltpu.VMEM((CH, planes, NY, NZ), BF16),
            pltpu.VMEM((CH * NY, NZ), F32),
            pltpu.SemaphoreType.DMA((2,)),
            pltpu.SemaphoreType.DMA,
            pltpu.SemaphoreType.DMA,
            pltpu.SemaphoreType.DMA((2,)),
            pltpu.SemaphoreType.DMA((2,)),
            pltpu.SemaphoreType.DMA((2,)),
            pltpu.SemaphoreType.DMA((2,)),
            pltpu.SemaphoreType.DMA,
            pltpu.SemaphoreType.DMA,
            pltpu.SemaphoreType.DMA,
            pltpu.SemaphoreType.DMA,
            pltpu.SemaphoreType.DMA,
            pltpu.SemaphoreType.DMA((2,)),
        ],
        compiler_params=pltpu.CompilerParams(
            collective_id=0, has_side_effects=True, vmem_limit_bytes=32 * 1024 * 1024
        ),
    )(grades, cotangent, wslot)
    total = total.reshape(rows, 8, 128)
    taps = jnp.concatenate(
        [total[:, :6].reshape(rows, 3, 256), total[:, 6, :96].reshape(rows, 3, 32)], axis=2
    )
    grad_weight = taps.reshape(rows, 3, 9, 32).transpose(0, 2, 1, 3).reshape(rows, 864)
    grad_bias = jnp.sum(total[:, 7], axis=1)
    return act, gin, grad_weight, grad_bias


def solution(mesh):
    real, strike = mesh.shape["real"], mesh.shape["strike"]
    co = 2
    xl = 2 if strike >= 8 else 1
    zs = strike // (xl * co)
    split = P("real", None, "strike", None, None)
    specs = (split, split, P("real", None), P("real"))
    body = functools.partial(local, real=real, xl=xl, zs=zs, co=co)
    return jax.shard_map(body, mesh=mesh, in_specs=specs, out_specs=specs, check_vma=False)
```

time: 315 us -> 47.7 us (0.15); the launches traced: 311 us -> 47.5 us
  blocking collectives: 170 us -> 0 us
  waiting for transfers between devices: 58.3 us -> 0 us
  Pallas kernels: 0 us -> 40.6 us
  matrix products: 31.7 us -> 0 us
  starting transfers between devices: 22.5 us -> 0 us
  between operations: 16.4 us -> 0.69 us
  other arithmetic: 4.62 us -> 0.72 us
    psum x1 -> x0, blocking collectives: 106 us -> none  [local(): summed = lax.psum((local_weight, local_bias), 'strike')]
    unnamed x2 -> x0, waiting for transfers between devices: 58.2 us -> none
    pallas_call x0 -> x1, Pallas kernels: none -> 40.6 us  [local(): pl.pallas_call(functools.partial(kernel, real, xl, zs, co, planes, factor...]
    unnamed x2 -> x0, blocking collectives: 35.5 us -> none
    dot_general x81 -> x0, matrix products: 31.7 us -> none  [the longest x27 11.4 us: local(): jnp.einsum('oi,ixyz->oxyz', kernel3[:, column, :], window, preferred_elem...]
    all_gather x1 -> x0, blocking collectives: 29 us -> none  [local(): lax.all_gather(weight, 'real', axis=0, tiled=True)]
    ppermute x4 -> x0, starting transfers between devices: 22.4 us -> none  [the longest x2 11.5 us: padded(): after = lax.ppermute(leading, axis, down)]
  transfers between devices with their start and end apart: 5 -> 0, of which waited for: 1 -> 0; matrix products, arithmetic and copies ran while one was open for 2% -> 0% of each run, Pallas kernels for 0% -> 0%
where the time goes in v1:
time: 47.7 us; the launch traced here: 47.5 us
  Pallas kernels  40.6 us (85%)
  local copies, waits for them, and re-layouts  5.47 us (11%)
  other arithmetic  0.72 us (2%)
  between operations  0.69 us (1%)
    pallas_call x1, Pallas kernels, local(): pl.pallas_call(functools.partial(kernel, real, xl, zs, co, planes, factor...  40.6 us
    unnamed x8, local copies, waits for them, and re-layouts  3.67 us

profile of v1, /device:TPU:1, one launch (start us, length us, event | category | flops | bytes accessed | tf_op | source)
XLA Modules:
  0.0 47.5 jit_solution(998730194023412553)
XLA Ops:
  0.6 0.0 copy-start.2
  0.7 0.1 pad.4.clone
  0.7 0.8 %copy.10 = bf16[4,1]{1,0:T(4,128)(2,1)S(1)} copy(bf16[4,1]{0,1:T(2,128)(2,1)} %bitcast.7) | data formatting | bytes 16 | tf_op jit(solution)/shard_map/broadcast_in_dim | solution.py:373
  1.5 0.0 copy-done.2
  1.5 0.1 maximum_maximum_fusion
  1.6 0.0 copy-start
  1.6 1.0 %copy-done = bf16[1,32,2,32,128]{4,3,2,1,0:T(8,128)(2,1)S(1)} copy-done((bf16[1,32,2,32,128]{4,3,2,1,0:T(8,128)(2,1)S(1)}, bf16[1,32,2,32,128]{4,3,2,1,0:T(8,128)(2,1)}, u32[]{:S(2)}) %copy-start) | copy-done | bytes 524312
  2.6 0.0 copy-start.1
  2.6 1.0 %copy-done.1 = bf16[1,32,2,32,128]{4,3,2,1,0:T(8,128)(2,1)S(1)} copy-done((bf16[1,32,2,32,128]{4,3,2,1,0:T(8,128)(2,1)S(1)}, bf16[1,32,2,32,128]{4,3,2,1,0:T(8,128)(2,1)}, u32[]{:S(2)}) %copy-start.1) | copy-done | bytes 524312
  3.7 40.6 %shard_map.75 = (bf16[1,32,2,32,128]{4,3,2,1,0:T(8,128)(2,1)S(1)}, bf16[1,32,2,32,128]{4,3,2,1,0:T(8,128)(2,1)S(1)}, f32[4,8,128]{2,1,0:T(8,128)S(1)}) custom-call(bf16[1,32,2,32,128]{4,3,2,1,0:T(8,128)(2,1)S(1)} %copy-done, bf16[1,32,2,32,128]{4,3,2,1,0:T(8,128)(2,1)S(1)} %copy-done.1, bf16[16,256]{1,0:T(8,128)(2,1)S(1)} %reshape.20.wslot), custom_call_target="tpu_custom_call" | custom-call | tf_op jit(solution)/shard_map/pallas_call | solution.py:378
  44.3 0.1 reshape_squeeze.3
  44.4 0.1 reshape.22
  44.6 0.7 %reshape.23 = f32[4,864]{1,0:T(4,128)} reshape(f32[4,9,3,32]{3,2,1,0:T(4,128)S(1)} %copy.12) | data formatting | bytes 27648 | tf_op jit(solution)/shard_map/reshape | solution.py:428
  45.3 0.6 %slice_reduce_fusion = f32[4]{0:T(128)} fusion(f32[4,8,128]{2,1,0:T(8,128)S(1)} %get-tuple-element.9), kind=kLoop, calls=%fused_computation.2 | loop fusion | flops 508 | bytes 2064 | tf_op jit(solution)/shard_map/reduce_sum | solution.py:429
  45.9 0.8 %copy.15 = bf16[1,32,2,32,128]{4,3,2,1,0:T(8,128)(2,1)} copy(bf16[1,32,2,32,128]{4,3,2,1,0:T(8,128)(2,1)S(1)} %get-tuple-element.14) | data formatting | bytes 1048576
  46.7 0.8 %copy.16 = bf16[1,32,2,32,128]{4,3,2,1,0:T(8,128)(2,1)} copy(bf16[1,32,2,32,128]{4,3,2,1,0:T(8,128)(2,1)S(1)} %get-tuple-element.15) | data formatting | bytes 1048576
  (7 shorter events, 0.1 us)
Async XLA Ops:
  0.6 0.9 %copy-start.2 = (bf16[4,864]{1,0:T(4,128)(2,1)S(1)}, bf16[4,864]{1,0:T(4,128)(2,1)}, u32[]{:S(2)}) copy-start(bf16[4,864]{1,0:T(4,128)(2,1)} %param.6) | copy-start | bytes 20740
  1.6 1.0 %copy-start = (bf16[1,32,2,32,128]{4,3,2,1,0:T(8,128)(2,1)S(1)}, bf16[1,32,2,32,128]{4,3,2,1,0:T(8,128)(2,1)}, u32[]{:S(2)}) copy-start(bf16[1,32,2,32,128]{4,3,2,1,0:T(8,128)(2,1)} %grades.1) | copy-start | bytes 1572868
  2.6 1.0 %copy-start.1 = (bf16[1,32,2,32,128]{4,3,2,1,0:T(8,128)(2,1)S(1)}, bf16[1,32,2,32,128]{4,3,2,1,0:T(8,128)(2,1)}, u32[]{:S(2)}) copy-start(bf16[1,32,2,32,128]{4,3,2,1,0:T(8,128)(2,1)} %cot.1) | copy-start | bytes 1572868

commit v2 on v1

--- a/solution.py
+++ b/solution.py
@@ -13,7 +13,7 @@
 CH = 32
 NY = 32
 NZ = 128
-WIDE = 4
+WIDE = 32
 
 
 def transpose_in(plane, work, put):
@@ -38,17 +38,15 @@
     cells = jnp.concatenate(pieces, axis=0)
     product = jnp.dot(weights[...], cells, preferred_element_type=F32)
     lane = lax.broadcasted_iota(jnp.int32, (CH, NZ), 1)
-    out = []
     for j in range(WIDE):
         part = product[:, j * NZ : (j + 1) * NZ]
         low = pltpu.roll(part[0:CH], 1, 1)
         high = pltpu.roll(part[2 * CH : 3 * CH], NZ - 1, 1)
-        out.append(
+        yield (
             part[CH : 2 * CH]
             + jnp.where(lane == 0, 0.0, low)
             + jnp.where(lane == NZ - 1, 0.0, high)
         )
-    return out
 
 
 def wait_for(ref, sem):
@@ -57,11 +55,11 @@
 
 def kernel(
     real, xl, zs, co, planes, factor,
-    grades, cot, wslot,
+    grades, cot, weight, bias,
     act_out, gin_out, sum_out,
-    gv, cv, work, field, dgrad, dshift, wf, wb, bias_col, slots, acc, bias_acc,
-    send1, recv1, recv2, piece, act_v, gin_v,
-    in_sem, w_send, w_recv, fs, fr, ds, dr, s1, r1, s2, r2, own_sem, out_sem,
+    gv, cv, wv, work, turned_out, field, dgrad, dshift, wslot, wf, wb, bias_col, slots, bias_acc,
+    send1, recv1, recv2, piece,
+    in_sem, w_send, w_recv, fs, fr, ds, dr, s1, r1, s2, r2, own_sem,
 ):
     strike = xl * zs * co
     quarter = xl * co
@@ -77,6 +75,8 @@
 
     load_g = pltpu.make_async_copy(grades.at[0], gv, in_sem.at[0])
     load_c = pltpu.make_async_copy(cot.at[0], cv, in_sem.at[1])
+    load_w = pltpu.make_async_copy(weight, wv, in_sem.at[2])
+    load_w.start()
     load_g.start()
     load_c.start()
 
@@ -120,6 +120,15 @@
         clear(field, planes + 1)
         clear(dgrad, planes + 1)
 
+    rows = CH // real
+    load_w.wait()
+    taps = wv[...].astype(F32)
+    last = jnp.concatenate(
+        [taps[:, 768:864], bias[...].astype(F32)[:, :32], jnp.zeros((rows, 128), F32)], axis=1
+    )
+    wslot[...] = jnp.concatenate(
+        [taps[:, 0:256], taps[:, 256:512], taps[:, 512:768], last], axis=0
+    ).astype(BF16)
     slots[me_r] = wslot[...]
     load_g.wait()
     for x in range(planes):
@@ -189,7 +198,10 @@
     gathered = slots[...].reshape(128, 256)
     row = lax.broadcasted_iota(jnp.int32, (128, 128), 0)
     col = lax.broadcasted_iota(jnp.int32, (128, 128), 1)
-    order = (col == lax.rem(row, CH) * 4 + row // CH).astype(BF16)
+    out_row, group = lax.rem(row, CH), row // CH
+    order = (
+        col == (out_row // rows) * (4 * rows) + group * rows + lax.rem(out_row, rows)
+    ).astype(BF16)
     whole = jnp.dot(order, gathered, preferred_element_type=F32)
     turned = jnp.concatenate([whole[:, :128].T, whole[:, 128:].T], axis=0)
     for c in range(3):
@@ -215,57 +227,47 @@
 
         lax.fori_loop(0, CH, spread, 0, unroll=8)
 
-        def forward(step, carry, x=x):
-            y0 = step * WIDE
-            for j, value in enumerate(stencil(field, wf, x, y0)):
-                pre = value + bias_col[...]
-                sig = jax.nn.sigmoid(pre)
-                gin_v[pl.ds(y0 + j, CH, NY), :] = pre * sig
-                upstream = work[pl.ds(y0 + j, CH, NY), :]
-                dpre = (upstream * sig * (1.0 + pre * (1.0 - sig))).astype(BF16)
-                dgrad[x + 1, y0 + j + 1] = dpre
-                wide = dpre.astype(F32)
-                bias_acc[...] += wide
-                before = jnp.where(lane == NZ - 1, 0.0, pltpu.roll(wide, NZ - 1, 1))
-                after = jnp.where(lane == 0, 0.0, pltpu.roll(wide, 1, 1))
-                dshift[x, y0 + j] = jnp.concatenate(
-                    [before.astype(BF16), dpre, after.astype(BF16)], axis=0
-                )
+        for y, value in enumerate(stencil(field, wf, x, 0)):
+            pre = value + bias_col[...]
+            sig = jax.nn.sigmoid(pre)
+            rise = pre * sig
+            turned_out[pl.ds(y, CH, NY), :] = rise
+            upstream = work[pl.ds(y, CH, NY), :]
+            dpre = (upstream * (sig + rise * (1.0 - sig))).astype(BF16)
+            dgrad[x + 1, y + 1] = dpre
+            wide = dpre.astype(F32)
+            bias_acc[...] += wide
+            before = jnp.where(lane == NZ - 1, 0.0, pltpu.roll(wide, NZ - 1, 1))
+            after = jnp.where(lane == 0, 0.0, pltpu.roll(wide, 1, 1))
+            dshift[x, y, 0:CH] = before.astype(BF16)
+            dshift[x, y, CH : 2 * CH] = dpre
+            dshift[x, y, 2 * CH : 3 * CH] = after.astype(BF16)
+
+        def pack(c, carry, x=x):
+            act_out[0, c, x] = turned_out[pl.ds(pl.multiple_of(c * NY, NY), NY), :].astype(BF16)
             return carry
 
-        lax.fori_loop(0, NY // WIDE, forward, 0)
-
-        def pack(c, carry, x=x):
-            act_v[c, x] = gin_v[pl.ds(pl.multiple_of(c * NY, NY), NY), :].astype(BF16)
-            return carry
-
         lax.fori_loop(0, CH, pack, 0, unroll=8)
 
     send_halo(dgrad, ds, dr)
-    store_act = pltpu.make_async_copy(act_v, act_out.at[0], out_sem.at[0])
-    store_act.start()
-
-    acc[...] = jnp.zeros_like(acc)
+    total = None
     for x in range(planes):
-
-        def gram(step, carry, x=x):
-            y0 = step * WIDE
-            left = jnp.concatenate([dshift[x, y0 + j] for j in range(WIDE)], axis=1)
-            pieces = []
-            for a in range(3):
-                for b in range(3):
-                    pieces.append(
-                        jnp.concatenate([field[x + a, y0 + j + b] for j in range(WIDE)], axis=1)
-                    )
-            right = jnp.concatenate(pieces, axis=0)
-            acc[...] += lax.dot_general(
-                left, right, (((1,), (1,)), ((), ())), preferred_element_type=F32
-            )
-            return carry
-
-        lax.fori_loop(0, NY // WIDE, gram, 0)
-
-    total = acc[...]
+        left = jnp.concatenate(
+            [
+                jnp.concatenate([field[x + a, y + b] for y in range(NY)], axis=1)
+                for a in range(3)
+                for b in range(3)
+            ],
+            axis=0,
+        )
+        right = jnp.concatenate([dshift[x, y] for y in range(NY)], axis=1)
+        part = lax.dot_general(left, right, (((1,), (1,)), ((), ())), preferred_element_type=F32)
+        total = part if total is None else total + part
+    total = jnp.concatenate([total, jnp.zeros((9 * CH, CH), F32)], axis=1)
+    total = jnp.concatenate([total, jnp.zeros((3 * CH, 4 * CH), F32)], axis=0)
+    total = jnp.concatenate(
+        [total[k * 128 : (k + 1) * 128].T for k in range(3)], axis=1
+    )
     tails = []
     for c in range(3):
         block = total[c * CH : (c + 1) * CH]
@@ -275,10 +277,10 @@
     send1[pl.ds(6, CH, 8), :] = jnp.concatenate(tails + [jnp.zeros((CH, 32), F32)], axis=1)
     send1[pl.ds(7, CH, 8), :] = bias_acc[...]
 
-    rows = per * 8
+    tile = per * 8
 
     def chunk(m):
-        return send1.at[pl.ds(pl.multiple_of(m * rows, 8), rows)]
+        return send1.at[pl.ds(pl.multiple_of(m * tile, 8), tile)]
 
     def scatter(k, carry):
         m = lax.rem(me_m + k, members)
@@ -296,22 +298,14 @@
     own = pltpu.make_async_copy(chunk(me_m), recv1.at[me_m], own_sem)
     own.start()
 
-    def turn_out(x, y, value):
-        gin_v[pl.ds(y, CH, NY), :] = value
-
     got_halo(dgrad, dr)
 
     def backward(x):
-        def step_of(step, carry):
-            y0 = step * WIDE
-            for j, value in enumerate(stencil(dgrad, wb, x, y0)):
-                gin_v[pl.ds(y0 + j, CH, NY), :] = value
-            return carry
-
-        lax.fori_loop(0, NY // WIDE, step_of, 0)
+        for y, value in enumerate(stencil(dgrad, wb, x, 0)):
+            turned_out[pl.ds(y, CH, NY), :] = value
 
         def pack(c, carry):
-            gv[c, x] = gin_v[pl.ds(pl.multiple_of(c * NY, NY), NY), :].astype(BF16)
+            gin_out[0, c, x] = turned_out[pl.ds(pl.multiple_of(c * NY, NY), NY), :].astype(BF16)
             return carry
 
         lax.fori_loop(0, CH, pack, 0, unroll=8)
@@ -341,8 +335,6 @@
 
     for x in range(1, planes):
         backward(x)
-    store_gin = pltpu.make_async_copy(gv, gin_out.at[0], out_sem.at[1])
-    store_gin.start()
 
     wait_for(recv2.at[pl.ds(0, strike - 1)], r2)
     for xi in range(xl):
@@ -350,15 +342,33 @@
             value = recv2[xi * zs * co + ci]
             for z in range(1, zs):
                 value = value + recv2[(xi * zs + z) * co + ci]
-            sum_out[xi * co + ci] = value * factor
+            sum_out[pl.ds((xi * co + ci) * tile, tile), :] = value * factor
 
     wait_for(slots.at[pl.ds(0, real - 1)], w_send)
     sent_halo(field, fs)
     sent_halo(dgrad, ds)
     wait_for(recv1.at[pl.ds(0, members - 1)], s1)
     wait_for(recv2.at[pl.ds(0, strike - 1)], s2)
-    store_act.wait()
-    store_gin.wait()
+
+
+def place(rows, act, gin, total, act_out, gin_out, weight_out, bias_out, sems):
+    move_act = pltpu.make_async_copy(act, act_out, sems.at[0])
+    move_gin = pltpu.make_async_copy(gin, gin_out, sems.at[1])
+    move_act.start()
+    move_gin.start()
+    parts = [total[pl.ds(g, rows, 8), :] for g in range(8)]
+    taps = []
+    for ab in range(9):
+        for c in range(3):
+            if ab < 8:
+                source, at = parts[2 * c + ab // 4], (ab % 4) * 32
+            else:
+                source, at = parts[6], c * 32
+            taps.append(source[:, at : at + 32])
+    weight_out[...] = jnp.concatenate(taps, axis=1)
+    bias_out[...] = jnp.sum(parts[7], axis=1, keepdims=True)
+    move_act.wait()
+    move_gin.wait()
 
 
 def local(grades, cotangent, weight, bias, *, real, xl, zs, co):
@@ -369,65 +379,60 @@
     rows = weight.shape[0]
     cells = real * strike * planes * NY * NZ
     factor = 1.0 / cells**0.5
-    wslot = jnp.concatenate(
-        [weight, bias[:, None], jnp.zeros((rows, 1024 - 865), BF16)], axis=1
-    ).reshape(rows * 4, 256)
-    hbm = pl.BlockSpec(memory_space=pl.ANY)
+    hbm = pl.BlockSpec(memory_space=pltpu.HBM)
     vmem = pl.BlockSpec(memory_space=pltpu.VMEM)
-    block = (1, CH, planes, NY, NZ)
+    block = jax.ShapeDtypeStruct((1, CH, planes, NY, NZ), BF16)
+    scratch = [
+        ((CH, planes, NY, NZ), BF16),
+        ((CH, planes, NY, NZ), BF16),
+        ((rows, 27 * CH), BF16),
+        ((CH * NY, NZ), F32),
+        ((CH * NY, NZ), F32),
+        ((planes + 2, NY + 2, CH, NZ), BF16),
+        ((planes + 2, NY + 2, CH, NZ), BF16),
+        ((planes, NY, 3 * CH, NZ), BF16),
+        ((rows * 4, 256), BF16),
+        ((3 * CH, 9 * CH), BF16),
+        ((3 * CH, 9 * CH), BF16),
+        ((CH, NZ), F32),
+        ((real, rows * 4, 256), BF16),
+        ((CH, NZ), F32),
+        ((CH * 8, 128), F32),
+        ((members, per * 8, 128), F32),
+        ((strike, per * 8, 128), F32),
+        ((per * 8, 128), F32),
+    ]
+    pair, single = pltpu.SemaphoreType.DMA((2,)), pltpu.SemaphoreType.DMA
     act, gin, total = pl.pallas_call(
         functools.partial(kernel, real, xl, zs, co, planes, factor),
-        out_shape=(
-            jax.ShapeDtypeStruct(block, BF16),
-            jax.ShapeDtypeStruct(block, BF16),
-            jax.ShapeDtypeStruct((xl * co, per * 8, 128), F32),
-        ),
-        in_specs=[hbm, hbm, vmem],
-        out_specs=(hbm, hbm, vmem),
-        scratch_shapes=[
-            pltpu.VMEM((CH, planes, NY, NZ), BF16),
-            pltpu.VMEM((CH, planes, NY, NZ), BF16),
-            pltpu.VMEM((CH * NY, NZ), F32),
-            pltpu.VMEM((planes + 2, NY + 2, CH, NZ), BF16),
-            pltpu.VMEM((planes + 2, NY + 2, CH, NZ), BF16),
-            pltpu.VMEM((planes, NY, 3 * CH, NZ), BF16),
-            pltpu.VMEM((3 * CH, 9 * CH), BF16),
-            pltpu.VMEM((3 * CH, 9 * CH), BF16),
-            pltpu.VMEM((CH, NZ), F32),
-            pltpu.VMEM((real, rows * 4, 256), BF16),
-            pltpu.VMEM((3 * CH, 9 * CH), F32),
-            pltpu.VMEM((CH, NZ), F32),
-            pltpu.VMEM((CH * 8, 128), F32),
-            pltpu.VMEM((members, per * 8, 128), F32),
-            pltpu.VMEM((strike, per * 8, 128), F32),
-            pltpu.VMEM((per * 8, 128), F32),
-            pltpu.VMEM((CH, planes, NY, NZ), BF16),
-            pltpu.VMEM((CH * NY, NZ), F32),
-            pltpu.SemaphoreType.DMA((2,)),
-            pltpu.SemaphoreType.DMA,
-            pltpu.SemaphoreType.DMA,
-            pltpu.SemaphoreType.DMA((2,)),
-            pltpu.SemaphoreType.DMA((2,)),
-            pltpu.SemaphoreType.DMA((2,)),
-            pltpu.SemaphoreType.DMA((2,)),
-            pltpu.SemaphoreType.DMA,
-            pltpu.SemaphoreType.DMA,
-            pltpu.SemaphoreType.DMA,
-            pltpu.SemaphoreType.DMA,
-            pltpu.SemaphoreType.DMA,
-            pltpu.SemaphoreType.DMA((2,)),
-        ],
+        out_shape=(block, block, jax.ShapeDtypeStruct((rows * 8, 128), F32)),
+        in_specs=[hbm, hbm, hbm, vmem],
+        out_specs=(vmem, vmem, vmem),
+        scratch_shapes=[pltpu.VMEM(*each) for each in scratch]
+        + [pltpu.SemaphoreType.DMA((3,)), single, single, pair, pair, pair, pair] + [single] * 5,
         compiler_params=pltpu.CompilerParams(
             collective_id=0, has_side_effects=True, vmem_limit_bytes=32 * 1024 * 1024
         ),
-    )(grades, cotangent, wslot)
-    total = total.reshape(rows, 8, 128)
-    taps = jnp.concatenate(
-        [total[:, :6].reshape(rows, 3, 256), total[:, 6, :96].reshape(rows, 3, 32)], axis=2
+    )(
+        pltpu.with_memory_space_constraint(grades, pltpu.HBM),
+        pltpu.with_memory_space_constraint(cotangent, pltpu.HBM),
+        pltpu.with_memory_space_constraint(weight, pltpu.HBM),
+        jnp.broadcast_to(bias[:, None], (rows, 128)),
     )
-    grad_weight = taps.reshape(rows, 3, 9, 32).transpose(0, 2, 1, 3).reshape(rows, 864)
-    grad_bias = jnp.sum(total[:, 7], axis=1)
-    return act, gin, grad_weight, grad_bias
+    act, gin, grad_weight, grad_bias = pl.pallas_call(
+        functools.partial(place, rows),
+        out_shape=(
+            block,
+            block,
+            jax.ShapeDtypeStruct((rows, 27 * CH), F32),
+            jax.ShapeDtypeStruct((rows, 1), F32),
+        ),
+        in_specs=[vmem, vmem, vmem],
+        out_specs=(hbm, hbm, vmem, vmem),
+        scratch_shapes=[pair],
+        compiler_params=pltpu.CompilerParams(vmem_limit_bytes=4 * 1024 * 1024),
+    )(act, gin, total)
+    return act, gin, grad_weight, grad_bias.reshape(rows)
 
 
 def solution(mesh):

time: 47.7 us -> 37.9 us (0.79)
  Pallas kernels: 40.6 us -> 35.8 us
  local copies, waits for them, and re-layouts: 5.47 us -> 0.73 us
    pallas_call x1, Pallas kernels: 40.6 us -> 34.2 us  [local(): pl.pallas_call(functools.partial(kernel, real, xl, zs, co, planes, factor...]
    unnamed x8 -> x0, local copies, waits for them, and re-layouts: 3.67 us -> none
    pallas_call x0 -> x1, Pallas kernels: none -> 1.59 us  [local(): pl.pallas_call(functools.partial(place, rows), out_shape=(block, block, j...]
    reshape x4 -> x0, local copies, waits for them, and re-layouts: 0.82 us -> none  [the longest x2 0.79 us: local(): taps.reshape(rows, 3, 9, 32).transpose(0, 2, 1, 3).reshape(rows, 864)]
    pallas_call x0 -> x1, other arithmetic: none -> 0.63 us  [local(): pl.pallas_call(functools.partial(place, rows), out_shape=(block, block, j...]
    reduce_sum x1 -> x0, other arithmetic: 0.62 us -> none  [local(): grad_bias = jnp.sum(total[:, 7], axis=1)]
where the time goes in v2:
time: 37.9 us; the launch traced here: 37.8 us
  Pallas kernels  35.8 us (94%)
  local copies, waits for them, and re-layouts  0.73 us (2%)
  between operations  0.65 us (2%)
  other arithmetic  0.63 us (2%)
    pallas_call x1, Pallas kernels, local(): pl.pallas_call(functools.partial(kernel, real, xl, zs, co, planes, factor...  34.2 us
    pallas_call x1, Pallas kernels, local(): pl.pallas_call(functools.partial(place, rows), out_shape=(block, block, j...  1.59 us

profile of v2, /device:TPU:1, one launch (start us, length us, event | category | flops | bytes accessed | tf_op | source)
XLA Modules:
  0.0 37.8 jit_solution(16056328343225593266)
XLA Ops:
  0.6 0.7 %broadcast_in_dim.2.bias = bf16[4,128]{1,0:T(4,128)(2,1)S(1)} broadcast(bf16[4]{0:T(256)(128)(2,1)} %param.7), dimensions={0} | broadcast | bytes 1032 | tf_op jit(solution)/shard_map/broadcast_in_dim | solution.py:420
  1.4 34.2 %shard_map.75 = (bf16[1,32,2,32,128]{4,3,2,1,0:T(8,128)(2,1)S(1)}, bf16[1,32,2,32,128]{4,3,2,1,0:T(8,128)(2,1)S(1)}, f32[32,128]{1,0:T(8,128)S(1)}) custom-call(bf16[1,32,2,32,128]{4,3,2,1,0:T(8,128)(2,1)} %grades.1, bf16[1,32,2,32,128]{4,3,2,1,0:T(8,128)(2,1)} %cot.1, bf16[4,864]{1,0:T(4,128)(2,1)} %weight.1, bf16[4,128]{1,0:T(4,128)(2,1)S(1)} %broadcast_in_dim.2.bias), custom_call_target="tpu_custom_call" | custom-call | tf_op jit(solution)/shard_map/pallas_call | solution.py:406
  35.6 1.6 %shard_map.76 = (bf16[1,32,2,32,128]{4,3,2,1,0:T(8,128)(2,1)}, bf16[1,32,2,32,128]{4,3,2,1,0:T(8,128)(2,1)}, f32[4,864]{1,0:T(4,128)}, f32[4,1]{1,0:T(4,128)S(1)}) custom-call(bf16[1,32,2,32,128]{4,3,2,1,0:T(8,128)(2,1)S(1)} %get-tuple-element.11.act, bf16[1,32,2,32,128]{4,3,2,1,0:T(8,128)(2,1)S(1)} %get-tuple-element.12.gin, ...), custom_call_target="tpu_custom_call" | custom-call | tf_op jit(solution)/shard_map/pallas_call | solution.py:422
  37.2 0.6 %reduce = f32[4]{0:T(128)} reduce(f32[4,1]{1,0:T(4,128)S(1)} %get-tuple-element.17, f32[]{:T(128)} %constant.4), dimensions={1}, to_apply=%get-tuple-element.17.reduce_sub_computation | reduce | bytes 36 | tf_op jit(solution)/shard_map/pallas_call | solution.py:422

commit v3 on v2

--- a/solution.py
+++ b/solution.py
@@ -13,7 +13,6 @@
 CH = 32
 NY = 32
 NZ = 128
-WIDE = 32
 
 
 def transpose_in(plane, work, put):
@@ -30,16 +29,17 @@
     lax.fori_loop(0, NY, gather, 0, unroll=8)
 
 
-def stencil(buf, weights, x, y0):
+def stencil(buf, weights, x, near):
     pieces = []
-    for a in range(3):
+    for a in near:
         for b in range(3):
-            pieces.append(jnp.concatenate([buf[x + a, y0 + j + b] for j in range(WIDE)], axis=1))
+            pieces.append(jnp.concatenate([buf[x + a, y + b] for y in range(NY)], axis=1))
     cells = jnp.concatenate(pieces, axis=0)
-    product = jnp.dot(weights[...], cells, preferred_element_type=F32)
+    columns = slice(near[0] * 3 * CH, (near[-1] + 1) * 3 * CH)
+    product = jnp.dot(weights[:, columns], cells, preferred_element_type=F32)
     lane = lax.broadcasted_iota(jnp.int32, (CH, NZ), 1)
-    for j in range(WIDE):
-        part = product[:, j * NZ : (j + 1) * NZ]
+    for y in range(NY):
+        part = product[:, y * NZ : (y + 1) * NZ]
         low = pltpu.roll(part[0:CH], 1, 1)
         high = pltpu.roll(part[2 * CH : 3 * CH], NZ - 1, 1)
         yield (
@@ -57,7 +57,7 @@
     real, xl, zs, co, planes, factor,
     grades, cot, weight, bias,
     act_out, gin_out, sum_out,
-    gv, cv, wv, work, turned_out, field, dgrad, dshift, wslot, wf, wb, bias_col, slots, bias_acc,
+    gv, cv, wv, bv, work, turned_out, partial, field, dgrad, dshift, wslot, wf, wb, bias_col, slots,
     send1, recv1, recv2, piece,
     in_sem, w_send, w_recv, fs, fr, ds, dr, s1, r1, s2, r2, own_sem,
 ):
@@ -76,7 +76,9 @@
     load_g = pltpu.make_async_copy(grades.at[0], gv, in_sem.at[0])
     load_c = pltpu.make_async_copy(cot.at[0], cv, in_sem.at[1])
     load_w = pltpu.make_async_copy(weight, wv, in_sem.at[2])
+    load_b = pltpu.make_async_copy(bias, bv, in_sem.at[3])
     load_w.start()
+    load_b.start()
     load_g.start()
     load_c.start()
 
@@ -122,9 +124,13 @@
 
     rows = CH // real
     load_w.wait()
+    load_b.wait()
     taps = wv[...].astype(F32)
+    here = lax.broadcasted_iota(jnp.int32, (rows, rows), 0)
+    there = lax.broadcasted_iota(jnp.int32, (rows, rows), 1)
+    diagonal = jnp.where(here == there, jnp.broadcast_to(bv[...].astype(F32), (rows, rows)), 0.0)
     last = jnp.concatenate(
-        [taps[:, 768:864], bias[...].astype(F32)[:, :32], jnp.zeros((rows, 128), F32)], axis=1
+        [taps[:, 768:864], diagonal, jnp.zeros((rows, 160 - rows), F32)], axis=1
     )
     wslot[...] = jnp.concatenate(
         [taps[:, 0:256], taps[:, 256:512], taps[:, 512:768], last], axis=0
@@ -140,13 +146,19 @@
 
     pl.semaphore_wait(barrier, members - 1 + strike - 1)
 
+    wide_y = real // 2
+    my_xh, my_y = me_r // wide_y, lax.rem(me_r, wide_y)
+
     def send_weight(k, carry):
+        across = k // wide_y
+        to_r = lax.rem(my_xh + across, 2) * wide_y + lax.rem(my_y + lax.rem(k, wide_y), wide_y)
+        to_s = lax.rem(my_x + across, xl) * (zs * co) + my_z * co + my_c
         pltpu.make_async_remote_copy(
             src_ref=wslot,
             dst_ref=slots.at[me_r],
             send_sem=w_send,
             recv_sem=w_recv,
-            device_id=(lax.rem(me_r + k, real), me_s),
+            device_id=(to_r, to_s),
             device_id_type=MESH,
         ).start()
         return carry
@@ -183,11 +195,12 @@
         def _():
             wait_for(buf.at[1, pl.ds(1, NY)], send.at[1])
 
-    def got_halo(buf, recv):
+    def got_below(buf, recv):
         @pl.when(me_s > 0)
         def _():
             wait_for(buf.at[0, pl.ds(1, NY)], recv.at[0])
 
+    def got_above(buf, recv):
         @pl.when(me_s < strike - 1)
         def _():
             wait_for(buf.at[planes + 1, pl.ds(1, NY)], recv.at[1])
@@ -203,22 +216,25 @@
         col == (out_row // rows) * (4 * rows) + group * rows + lax.rem(out_row, rows)
     ).astype(BF16)
     whole = jnp.dot(order, gathered, preferred_element_type=F32)
-    turned = jnp.concatenate([whole[:, :128].T, whole[:, 128:].T], axis=0)
     for c in range(3):
-        ahead, back = [], []
+        ahead = []
         for ab in range(9):
             t = 3 * ab + c
             ahead.append(whole[(t // 8) * CH : (t // 8 + 1) * CH, (t % 8) * CH : (t % 8 + 1) * CH])
-            t = 26 - t
-            back.append(turned[(t % 8) * CH : (t % 8 + 1) * CH, (t // 8) * CH : (t // 8 + 1) * CH])
         wf[pl.ds(c * CH, CH), :] = jnp.concatenate(ahead, axis=1).astype(BF16)
-        wb[pl.ds(c * CH, CH), :] = jnp.concatenate(back, axis=1).astype(BF16)
-    bias_col[...] = jnp.broadcast_to(whole[96:128, 96:97], (CH, NZ))
+    bias_col[...] = jnp.broadcast_to(
+        jnp.sum(whole[96:128, 96 : 96 + rows], axis=1, keepdims=True), (CH, NZ)
+    )
+
+    lane = lax.broadcasted_iota(jnp.int32, (CH, NZ), 1)
+    sides = ((1, 2), (0, 1))
+    edges = ((0,), (2,))
+    for x in range(planes):
+        for y, value in enumerate(stencil(field, wf, x, sides[x])):
+            partial[x, y] = value + bias_col[...]
 
     load_c.wait()
-    bias_acc[...] = jnp.zeros_like(bias_acc)
-    got_halo(field, fr)
-    lane = lax.broadcasted_iota(jnp.int32, (CH, NZ), 1)
+    bias_sum = jnp.zeros((CH, NZ), F32)
     for x in range(planes):
 
         def spread(c, carry, x=x):
@@ -226,28 +242,22 @@
             return carry
 
         lax.fori_loop(0, CH, spread, 0, unroll=8)
-
-        for y, value in enumerate(stencil(field, wf, x, 0)):
-            pre = value + bias_col[...]
+        (got_below if x == 0 else got_above)(field, fr)
+        for y, value in enumerate(stencil(field, wf, x, edges[x])):
+            pre = value + partial[x, y]
             sig = jax.nn.sigmoid(pre)
             rise = pre * sig
-            turned_out[pl.ds(y, CH, NY), :] = rise
+            turned_out[pl.ds(x * CH * NY + y, CH, NY), :] = rise
             upstream = work[pl.ds(y, CH, NY), :]
             dpre = (upstream * (sig + rise * (1.0 - sig))).astype(BF16)
             dgrad[x + 1, y + 1] = dpre
             wide = dpre.astype(F32)
-            bias_acc[...] += wide
+            bias_sum = bias_sum + wide
             before = jnp.where(lane == NZ - 1, 0.0, pltpu.roll(wide, NZ - 1, 1))
             after = jnp.where(lane == 0, 0.0, pltpu.roll(wide, 1, 1))
             dshift[x, y, 0:CH] = before.astype(BF16)
             dshift[x, y, CH : 2 * CH] = dpre
             dshift[x, y, 2 * CH : 3 * CH] = after.astype(BF16)
-
-        def pack(c, carry, x=x):
-            act_out[0, c, x] = turned_out[pl.ds(pl.multiple_of(c * NY, NY), NY), :].astype(BF16)
-            return carry
-
-        lax.fori_loop(0, CH, pack, 0, unroll=8)
 
     send_halo(dgrad, ds, dr)
     total = None
@@ -275,7 +285,7 @@
         send1[pl.ds(2 * c + 1, CH, 8), :] = block[:, 128:256]
         tails.append(block[:, 256:288])
     send1[pl.ds(6, CH, 8), :] = jnp.concatenate(tails + [jnp.zeros((CH, 32), F32)], axis=1)
-    send1[pl.ds(7, CH, 8), :] = bias_acc[...]
+    send1[pl.ds(7, CH, 8), :] = bias_sum
 
     tile = per * 8
 
@@ -298,27 +308,35 @@
     own = pltpu.make_async_copy(chunk(me_m), recv1.at[me_m], own_sem)
     own.start()
 
-    got_halo(dgrad, dr)
-
-    def backward(x):
-        for y, value in enumerate(stencil(dgrad, wb, x, 0)):
-            turned_out[pl.ds(y, CH, NY), :] = value
-
-        def pack(c, carry):
-            gin_out[0, c, x] = turned_out[pl.ds(pl.multiple_of(c * NY, NY), NY), :].astype(BF16)
-            return carry
-
-        lax.fori_loop(0, CH, pack, 0, unroll=8)
-
-    backward(0)
+    def pack(out):
+        for x in range(planes):
+
+            def channel(c, carry, x=x):
+                rows_of = pl.ds(pl.multiple_of(x * CH * NY + c * NY, NY), NY)
+                out[0, c, x] = turned_out[rows_of, :].astype(BF16)
+                return carry
+
+            lax.fori_loop(0, CH, channel, 0, unroll=8)
+
+    pack(act_out)
+    turned = jnp.concatenate([whole[:, :128].T, whole[:, 128:].T], axis=0)
+    for c in range(3):
+        back = []
+        for ab in range(9):
+            t = 26 - (3 * ab + c)
+            back.append(turned[(t % 8) * CH : (t % 8 + 1) * CH, (t // 8) * CH : (t // 8 + 1) * CH])
+        wb[pl.ds(c * CH, CH), :] = jnp.concatenate(back, axis=1).astype(BF16)
+    for x in range(planes):
+        for y, value in enumerate(stencil(dgrad, wb, x, sides[x])):
+            partial[x, y] = value
 
     own.wait()
     wait_for(recv1.at[pl.ds(0, members - 1)], r1)
     plane_sum = recv1[0]
     for m in range(1, members):
         plane_sum = plane_sum + recv1[m]
-    piece[...] = plane_sum
-    recv2[me_s] = plane_sum
+    piece[...] = plane_sum.astype(BF16)
+    recv2[me_s] = plane_sum.astype(BF16)
 
     def spread_sum(k, carry):
         pltpu.make_async_remote_copy(
@@ -333,15 +351,18 @@
 
     lax.fori_loop(1, strike, spread_sum, 0)
 
-    for x in range(1, planes):
-        backward(x)
+    for x in range(planes):
+        (got_below if x == 0 else got_above)(dgrad, dr)
+        for y, value in enumerate(stencil(dgrad, wb, x, edges[x])):
+            turned_out[pl.ds(x * CH * NY + y, CH, NY), :] = value + partial[x, y]
+    pack(gin_out)
 
     wait_for(recv2.at[pl.ds(0, strike - 1)], r2)
     for xi in range(xl):
         for ci in range(co):
-            value = recv2[xi * zs * co + ci]
+            value = recv2[xi * zs * co + ci].astype(F32)
             for z in range(1, zs):
-                value = value + recv2[(xi * zs + z) * co + ci]
+                value = value + recv2[(xi * zs + z) * co + ci].astype(F32)
             sum_out[pl.ds((xi * co + ci) * tile, tile), :] = value * factor
 
     wait_for(slots.at[pl.ds(0, real - 1)], w_send)
@@ -351,11 +372,13 @@
     wait_for(recv2.at[pl.ds(0, strike - 1)], s2)
 
 
-def place(rows, act, gin, total, act_out, gin_out, weight_out, bias_out, sems):
-    move_act = pltpu.make_async_copy(act, act_out, sems.at[0])
-    move_gin = pltpu.make_async_copy(gin, gin_out, sems.at[1])
-    move_act.start()
-    move_gin.start()
+def place(rows, act, gin, total, act_out, gin_out, weight_out, bias_out, taps_v, sums_v, sems):
+    results = ((act, act_out), (gin, gin_out), (taps_v, weight_out), (sums_v, bias_out))
+    moves = [
+        pltpu.make_async_copy(held, out, sems.at[i]) for i, (held, out) in enumerate(results)
+    ]
+    moves[0].start()
+    moves[1].start()
     parts = [total[pl.ds(g, rows, 8), :] for g in range(8)]
     taps = []
     for ab in range(9):
@@ -365,10 +388,16 @@
             else:
                 source, at = parts[6], c * 32
             taps.append(source[:, at : at + 32])
-    weight_out[...] = jnp.concatenate(taps, axis=1)
-    bias_out[...] = jnp.sum(parts[7], axis=1, keepdims=True)
-    move_act.wait()
-    move_gin.wait()
+    taps_v[...] = jnp.concatenate(taps, axis=1)
+    sums = jnp.broadcast_to(jnp.sum(parts[7], axis=1, keepdims=True), (rows, 128))
+    here = lax.broadcasted_iota(jnp.int32, (rows, 128), 0)
+    there = lax.broadcasted_iota(jnp.int32, (rows, 128), 1)
+    line = jnp.sum(jnp.where(here == there, sums, 0.0), axis=0, keepdims=True)
+    sums_v[...] = line[:, :rows]
+    moves[2].start()
+    moves[3].start()
+    for move in moves:
+        move.wait()
 
 
 def local(grades, cotangent, weight, bias, *, real, xl, zs, co):
@@ -386,8 +415,10 @@
         ((CH, planes, NY, NZ), BF16),
         ((CH, planes, NY, NZ), BF16),
         ((rows, 27 * CH), BF16),
+        ((1, rows), BF16),
         ((CH * NY, NZ), F32),
-        ((CH * NY, NZ), F32),
+        ((planes * CH * NY, NZ), F32),
+        ((planes, NY, CH, NZ), F32),
         ((planes + 2, NY + 2, CH, NZ), BF16),
         ((planes + 2, NY + 2, CH, NZ), BF16),
         ((planes, NY, 3 * CH, NZ), BF16),
@@ -396,20 +427,19 @@
         ((3 * CH, 9 * CH), BF16),
         ((CH, NZ), F32),
         ((real, rows * 4, 256), BF16),
-        ((CH, NZ), F32),
         ((CH * 8, 128), F32),
         ((members, per * 8, 128), F32),
-        ((strike, per * 8, 128), F32),
-        ((per * 8, 128), F32),
+        ((strike, per * 8, 128), BF16),
+        ((per * 8, 128), BF16),
     ]
     pair, single = pltpu.SemaphoreType.DMA((2,)), pltpu.SemaphoreType.DMA
     act, gin, total = pl.pallas_call(
         functools.partial(kernel, real, xl, zs, co, planes, factor),
         out_shape=(block, block, jax.ShapeDtypeStruct((rows * 8, 128), F32)),
-        in_specs=[hbm, hbm, hbm, vmem],
+        in_specs=[hbm, hbm, hbm, hbm],
         out_specs=(vmem, vmem, vmem),
         scratch_shapes=[pltpu.VMEM(*each) for each in scratch]
-        + [pltpu.SemaphoreType.DMA((3,)), single, single, pair, pair, pair, pair] + [single] * 5,
+        + [pltpu.SemaphoreType.DMA((4,)), single, single, pair, pair, pair, pair] + [single] * 5,
         compiler_params=pltpu.CompilerParams(
             collective_id=0, has_side_effects=True, vmem_limit_bytes=32 * 1024 * 1024
         ),
@@ -417,7 +447,7 @@
         pltpu.with_memory_space_constraint(grades, pltpu.HBM),
         pltpu.with_memory_space_constraint(cotangent, pltpu.HBM),
         pltpu.with_memory_space_constraint(weight, pltpu.HBM),
-        jnp.broadcast_to(bias[:, None], (rows, 128)),
+        pltpu.with_memory_space_constraint(bias.reshape(1, rows), pltpu.HBM),
     )
     act, gin, grad_weight, grad_bias = pl.pallas_call(
         functools.partial(place, rows),
@@ -425,11 +455,15 @@
             block,
             block,
             jax.ShapeDtypeStruct((rows, 27 * CH), F32),
-            jax.ShapeDtypeStruct((rows, 1), F32),
+            jax.ShapeDtypeStruct((1, rows), F32),
         ),
         in_specs=[vmem, vmem, vmem],
-        out_specs=(hbm, hbm, vmem, vmem),
-        scratch_shapes=[pair],
+        out_specs=(hbm, hbm, hbm, hbm),
+        scratch_shapes=[
+            pltpu.VMEM((rows, 27 * CH), F32),
+            pltpu.VMEM((1, rows), F32),
+            pltpu.SemaphoreType.DMA((4,)),
+        ],
         compiler_params=pltpu.CompilerParams(vmem_limit_bytes=4 * 1024 * 1024),
     )(act, gin, total)
     return act, gin, grad_weight, grad_bias.reshape(rows)

time: 37.9 us -> 34.7 us (0.916)
  Pallas kernels: 35.8 us -> 33.9 us
  local copies, waits for them, and re-layouts: 0.73 us -> 0 us
  other arithmetic: 0.63 us -> 0 us
    pallas_call x1, Pallas kernels: 34.2 us -> 32.9 us  [local(): pl.pallas_call(functools.partial(kernel, real, xl, zs, co, planes, factor...]
    broadcast_in_dim x1 -> x0, local copies, waits for them, and re-layouts: 0.73 us -> none  [local(): jnp.broadcast_to(bias[:, None], (rows, 128))]
    pallas_call x1 -> x0, other arithmetic: 0.63 us -> none  [local(): pl.pallas_call(functools.partial(place, rows), out_shape=(block, block, j...]
    pallas_call x1, Pallas kernels: 1.59 us -> 1.01 us  [local(): pl.pallas_call(functools.partial(place, rows), out_shape=(block, block, j...]
where the time goes in v3:
time: 34.7 us; the launch traced here: 34.6 us
  Pallas kernels  33.9 us (98%)
  between operations  0.64 us (2%)
    pallas_call x1, Pallas kernels, local(): pl.pallas_call(functools.partial(kernel, real, xl, zs, co, planes, factor...  32.9 us
    pallas_call x1, Pallas kernels, local(): pl.pallas_call(functools.partial(place, rows), out_shape=(block, block, j...  1.01 us

profile of v3, /device:TPU:1, one launch (start us, length us, event | category | flops | bytes accessed | tf_op | source)
XLA Modules:
  0.0 34.6 jit_solution(10421188833236121586)
XLA Ops:
  0.6 32.9 %shard_map.75 = (bf16[1,32,2,32,128]{4,3,2,1,0:T(8,128)(2,1)S(1)}, bf16[1,32,2,32,128]{4,3,2,1,0:T(8,128)(2,1)S(1)}, f32[32,128]{1,0:T(8,128)S(1)}) custom-call(bf16[1,32,2,32,128]{4,3,2,1,0:T(8,128)(2,1)} %grades.1, bf16[1,32,2,32,128]{4,3,2,1,0:T(8,128)(2,1)} %cot.1, bf16[4,864]{1,0:T(4,128)(2,1)} %weight.1, bf16[1,4]{1,0:T(2,128)(2,1)} %bitcast.2), custom_call_target="tpu_custom_call" | custom-call | tf_op jit(solution)/shard_map/pallas_call | solution.py:436
  33.6 1.0 %shard_map.76 = (bf16[1,32,2,32,128]{4,3,2,1,0:T(8,128)(2,1)}, bf16[1,32,2,32,128]{4,3,2,1,0:T(8,128)(2,1)}, f32[4,864]{1,0:T(4,128)}, f32[1,4]{1,0:T(1,128)}) custom-call(bf16[1,32,2,32,128]{4,3,2,1,0:T(8,128)(2,1)S(1)} %get-tuple-element.11.act, bf16[1,32,2,32,128]{4,3,2,1,0:T(8,128)(2,1)S(1)} %get-tuple-element.12.gin, f32[32,128]{1,0:T(8,128)S(1)} %get-tuple-element.13.total), custom_call_target="tpu_custom_call" | custom-call | tf_op jit(solution)/shard_map/pallas_call | solution.py:452

commit v4 on v3

--- a/solution.py
+++ b/solution.py
@@ -59,7 +59,7 @@
     act_out, gin_out, sum_out,
     gv, cv, wv, bv, work, turned_out, partial, field, dgrad, dshift, wslot, wf, wb, bias_col, slots,
     send1, recv1, recv2, piece,
-    in_sem, w_send, w_recv, fs, fr, ds, dr, s1, r1, s2, r2, own_sem,
+    in_sem, w_send, w_recv, fs, fr, ds, dr, s1, r1, s2, r2, own_sem, seen1, seen2, seen3,
 ):
     strike = xl * zs * co
     quarter = xl * co
@@ -84,20 +84,38 @@
 
     barrier = pltpu.get_barrier_semaphore()
 
-    def greet_plane(k, carry):
-        pl.semaphore_signal(
-            barrier, inc=1, device_id=member(lax.rem(me_m + k, members)), device_id_type=MESH
-        )
-        return carry
-
-    def greet_strike(k, carry):
-        pl.semaphore_signal(
-            barrier, inc=1, device_id=(me_r, lax.rem(me_s + k, strike)), device_id_type=MESH
-        )
-        return carry
-
-    lax.fori_loop(1, members, greet_plane, 0)
-    lax.fori_loop(1, strike, greet_strike, 0)
+    wide_y = real // 2
+    my_xh, my_y = me_r // wide_y, lax.rem(me_r, wide_y)
+
+    def holder(k):
+        across = k // wide_y
+        to_r = lax.rem(my_xh + across, 2) * wide_y + lax.rem(my_y + lax.rem(k, wide_y), wide_y)
+        return to_r, lax.rem(my_x + across, xl) * (zs * co) + my_z * co + my_c
+
+    def beside(k):
+        q = lax.rem(my_x * co + my_c + k, quarter)
+        return me_r, (q // co) * (zs * co) + my_z * co + lax.rem(q, co)
+
+    def along(k):
+        return me_r, my_x * (zs * co) + lax.rem(my_z + k, zs) * co + my_c
+
+    def tell(sem, device):
+        pl.semaphore_signal(sem, inc=1, device_id=device, device_id_type=MESH)
+
+    for k in range(1, real):
+        tell(barrier, holder(k))
+    for k in range(1, quarter):
+        tell(barrier, beside(k))
+    for k in (1, zs - 1):
+        tell(barrier, along(k))
+
+    @pl.when(me_s < strike - 1)
+    def _():
+        tell(barrier, (me_r, me_s + 1))
+
+    @pl.when(me_s > 0)
+    def _():
+        tell(barrier, (me_r, me_s - 1))
 
     zero = jnp.zeros((CH, NZ), BF16)
     for x in range(planes + 2):
@@ -144,21 +162,19 @@
 
         transpose_in(lambda c, x=x: gv[c, x], work, put)
 
-    pl.semaphore_wait(barrier, members - 1 + strike - 1)
-
-    wide_y = real // 2
-    my_xh, my_y = me_r // wide_y, lax.rem(me_r, wide_y)
+    ends = (me_s == 0).astype(jnp.int32) + (me_s == strike - 1).astype(jnp.int32)
+    pl.semaphore_wait(barrier, real - 1 + quarter - 1 + 4 - ends)
+
+    for k in (1, zs - 1):
+        tell(seen1, along(k))
 
     def send_weight(k, carry):
-        across = k // wide_y
-        to_r = lax.rem(my_xh + across, 2) * wide_y + lax.rem(my_y + lax.rem(k, wide_y), wide_y)
-        to_s = lax.rem(my_x + across, xl) * (zs * co) + my_z * co + my_c
         pltpu.make_async_remote_copy(
             src_ref=wslot,
             dst_ref=slots.at[me_r],
             send_sem=w_send,
             recv_sem=w_recv,
-            device_id=(to_r, to_s),
+            device_id=holder(k),
             device_id_type=MESH,
         ).start()
         return carry
@@ -206,6 +222,10 @@
             wait_for(buf.at[planes + 1, pl.ds(1, NY)], recv.at[1])
 
     send_halo(field, fs, fr)
+
+    pl.semaphore_wait(seen1, 2)
+    for k in (2, zs - 2):
+        tell(seen2, along(k))
 
     wait_for(slots.at[pl.ds(0, real - 1)], w_recv)
     gathered = slots[...].reshape(128, 256)
@@ -232,6 +252,10 @@
     for x in range(planes):
         for y, value in enumerate(stencil(field, wf, x, sides[x])):
             partial[x, y] = value + bias_col[...]
+
+    pl.semaphore_wait(seen2, 2)
+    for k in range(1, quarter):
+        tell(seen3, beside(k))
 
     load_c.wait()
     bias_sum = jnp.zeros((CH, NZ), F32)
@@ -337,6 +361,8 @@
         plane_sum = plane_sum + recv1[m]
     piece[...] = plane_sum.astype(BF16)
     recv2[me_s] = plane_sum.astype(BF16)
+
+    pl.semaphore_wait(seen3, quarter - 1)
 
     def spread_sum(k, carry):
         pltpu.make_async_remote_copy(
@@ -439,7 +465,8 @@
         in_specs=[hbm, hbm, hbm, hbm],
         out_specs=(vmem, vmem, vmem),
         scratch_shapes=[pltpu.VMEM(*each) for each in scratch]
-        + [pltpu.SemaphoreType.DMA((4,)), single, single, pair, pair, pair, pair] + [single] * 5,
+        + [pltpu.SemaphoreType.DMA((4,)), single, single, pair, pair, pair, pair] + [single] * 5
+        + [pltpu.SemaphoreType.REGULAR] * 3,
         compiler_params=pltpu.CompilerParams(
             collective_id=0, has_side_effects=True, vmem_limit_bytes=32 * 1024 * 1024
         ),

time: 34.7 us -> 33.2 us (0.957)
  Pallas kernels: 33.9 us -> 32.4 us
    pallas_call x1, Pallas kernels: 32.9 us -> 31.4 us  [local(): pl.pallas_call(functools.partial(kernel, real, xl, zs, co, planes, factor...]
where the time goes in v4:
time: 33.2 us; the launch traced here: 33.1 us
  Pallas kernels  32.4 us (98%)
  between operations  0.64 us (2%)
    pallas_call x1, Pallas kernels, local(): pl.pallas_call(functools.partial(kernel, real, xl, zs, co, planes, factor...  31.4 us
    pallas_call x1, Pallas kernels, local(): pl.pallas_call(functools.partial(place, rows), out_shape=(block, block, j...  1.01 us

profile of v4, /device:TPU:1, one launch (start us, length us, event | category | flops | bytes accessed | tf_op | source)
XLA Modules:
  0.0 33.1 jit_solution(18095707162566287214)
XLA Ops:
  0.6 31.4 %shard_map.75 = (bf16[1,32,2,32,128]{4,3,2,1,0:T(8,128)(2,1)S(1)}, bf16[1,32,2,32,128]{4,3,2,1,0:T(8,128)(2,1)S(1)}, f32[32,128]{1,0:T(8,128)S(1)}) custom-call(bf16[1,32,2,32,128]{4,3,2,1,0:T(8,128)(2,1)} %grades.1, bf16[1,32,2,32,128]{4,3,2,1,0:T(8,128)(2,1)} %cot.1, bf16[4,864]{1,0:T(4,128)(2,1)} %weight.1, bf16[1,4]{1,0:T(2,128)(2,1)} %bitcast.2), custom_call_target="tpu_custom_call" | custom-call | tf_op jit(solution)/shard_map/pallas_call | solution.py:462
  32.1 1.0 %shard_map.76 = (bf16[1,32,2,32,128]{4,3,2,1,0:T(8,128)(2,1)}, bf16[1,32,2,32,128]{4,3,2,1,0:T(8,128)(2,1)}, f32[4,864]{1,0:T(4,128)}, f32[1,4]{1,0:T(1,128)}) custom-call(bf16[1,32,2,32,128]{4,3,2,1,0:T(8,128)(2,1)S(1)} %get-tuple-element.11.act, bf16[1,32,2,32,128]{4,3,2,1,0:T(8,128)(2,1)S(1)} %get-tuple-element.12.gin, f32[32,128]{1,0:T(8,128)S(1)} %get-tuple-element.13.total), custom_call_target="tpu_custom_call" | custom-call | tf_op jit(solution)/shard_map/pallas_call | solution.py:479

commit v5 on v4

--- a/solution.py
+++ b/solution.py
@@ -29,24 +29,49 @@
     lax.fori_loop(0, NY, gather, 0, unroll=8)
 
 
-def stencil(buf, weights, x, near):
+def rows_of(buf, slabs):
     pieces = []
-    for a in near:
+    for slab in slabs:
         for b in range(3):
-            pieces.append(jnp.concatenate([buf[x + a, y + b] for y in range(NY)], axis=1))
-    cells = jnp.concatenate(pieces, axis=0)
-    columns = slice(near[0] * 3 * CH, (near[-1] + 1) * 3 * CH)
-    product = jnp.dot(weights[:, columns], cells, preferred_element_type=F32)
+            pieces.append(jnp.concatenate([buf[slab, y + b] for y in range(NY)], axis=1))
+    return jnp.concatenate(pieces, axis=0)
+
+
+def gathered_z(part):
     lane = lax.broadcasted_iota(jnp.int32, (CH, NZ), 1)
+    low = pltpu.roll(part[0:CH], 1, 1)
+    high = pltpu.roll(part[2 * CH : 3 * CH], NZ - 1, 1)
+    return (
+        part[CH : 2 * CH]
+        + jnp.where(lane == 0, 0.0, low)
+        + jnp.where(lane == NZ - 1, 0.0, high)
+    )
+
+
+def inner_sums(buf, weights, partial, shift):
+    product = jnp.dot(weights[...], rows_of(buf, (1, 2)), preferred_element_type=F32)
+    for x in range(2):
+        for y in range(NY):
+            part = product[x * 3 * CH : (x + 1) * 3 * CH, y * NZ : (y + 1) * NZ]
+            value = gathered_z(part)
+            partial[x, y] = value if shift is None else value + shift
+
+
+def outer_sums(buf, weights, x):
+    product = jnp.dot(weights[x], rows_of(buf, (x * 3,)), preferred_element_type=F32)
     for y in range(NY):
-        part = product[:, y * NZ : (y + 1) * NZ]
-        low = pltpu.roll(part[0:CH], 1, 1)
-        high = pltpu.roll(part[2 * CH : 3 * CH], NZ - 1, 1)
-        yield (
-            part[CH : 2 * CH]
-            + jnp.where(lane == 0, 0.0, low)
-            + jnp.where(lane == NZ - 1, 0.0, high)
-        )
+        yield gathered_z(product[:, y * NZ : (y + 1) * NZ])
+
+
+def lay_out(block, inner, outer):
+    for c in range(3):
+        taps = [block(c, ab) for ab in range(9)]
+        for x in range(2):
+            rows = pl.ds((x * 3 + c) * CH, CH)
+            inner[rows, :] = jnp.concatenate(taps[3 - 3 * x : 9 - 3 * x], axis=1).astype(BF16)
+            outer[x, pl.ds(c * CH, CH), :] = jnp.concatenate(
+                taps[6 * x : 6 * x + 3], axis=1
+            ).astype(BF16)
 
 
 def wait_for(ref, sem):
@@ -57,7 +82,8 @@
     real, xl, zs, co, planes, factor,
     grades, cot, weight, bias,
     act_out, gin_out, sum_out,
-    gv, cv, wv, bv, work, turned_out, partial, field, dgrad, dshift, wslot, wf, wb, bias_col, slots,
+    gv, cv, wv, bv, work, upstream, turned_out, partial, field, dgrad, dshift, wslot,
+    wf_in, wf_out, wb_in, wb_out, bias_col, slots,
     send1, recv1, recv2, piece,
     in_sem, w_send, w_recv, fs, fr, ds, dr, s1, r1, s2, r2, own_sem, seen1, seen2, seen3,
 ):
@@ -211,17 +237,15 @@
         def _():
             wait_for(buf.at[1, pl.ds(1, NY)], send.at[1])
 
-    def got_below(buf, recv):
-        @pl.when(me_s > 0)
-        def _():
-            wait_for(buf.at[0, pl.ds(1, NY)], recv.at[0])
-
-    def got_above(buf, recv):
-        @pl.when(me_s < strike - 1)
-        def _():
-            wait_for(buf.at[planes + 1, pl.ds(1, NY)], recv.at[1])
-
     send_halo(field, fs, fr)
+
+    load_c.wait()
+    for x in range(planes):
+
+        def put_cot(y, value, x=x):
+            upstream[x, y] = value.astype(BF16)
+
+        transpose_in(lambda c, x=x: cv[c, x], work, put_cot)
 
     pl.semaphore_wait(seen1, 2)
     for k in (2, zs - 2):
@@ -236,44 +260,44 @@
         col == (out_row // rows) * (4 * rows) + group * rows + lax.rem(out_row, rows)
     ).astype(BF16)
     whole = jnp.dot(order, gathered, preferred_element_type=F32)
-    for c in range(3):
-        ahead = []
-        for ab in range(9):
-            t = 3 * ab + c
-            ahead.append(whole[(t // 8) * CH : (t // 8 + 1) * CH, (t % 8) * CH : (t % 8 + 1) * CH])
-        wf[pl.ds(c * CH, CH), :] = jnp.concatenate(ahead, axis=1).astype(BF16)
+    def forward_tap(c, ab):
+        t = 3 * ab + c
+        return whole[(t // 8) * CH : (t // 8 + 1) * CH, (t % 8) * CH : (t % 8 + 1) * CH]
+
+    lay_out(forward_tap, wf_in, wf_out)
     bias_col[...] = jnp.broadcast_to(
         jnp.sum(whole[96:128, 96 : 96 + rows], axis=1, keepdims=True), (CH, NZ)
     )
 
     lane = lax.broadcasted_iota(jnp.int32, (CH, NZ), 1)
-    sides = ((1, 2), (0, 1))
-    edges = ((0,), (2,))
-    for x in range(planes):
-        for y, value in enumerate(stencil(field, wf, x, sides[x])):
-            partial[x, y] = value + bias_col[...]
+    inner_sums(field, wf_in, partial, bias_col[...])
 
     pl.semaphore_wait(seen2, 2)
     for k in range(1, quarter):
         tell(seen3, beside(k))
 
-    load_c.wait()
-    bias_sum = jnp.zeros((CH, NZ), F32)
-    for x in range(planes):
-
-        def spread(c, carry, x=x):
-            work[pl.ds(pl.multiple_of(c * NY, NY), NY), :] = cv[c, x].astype(F32)
-            return carry
-
-        lax.fori_loop(0, CH, spread, 0, unroll=8)
-        (got_below if x == 0 else got_above)(field, fr)
-        for y, value in enumerate(stencil(field, wf, x, edges[x])):
+    def side(step):
+        return lax.rem(step + 1 + my_c, 2)
+
+    def got(buf, recv, x):
+        @pl.when((x == 0) & (me_s > 0))
+        def _():
+            wait_for(buf.at[0, pl.ds(1, NY)], recv.at[0])
+
+        @pl.when((x == 1) & (me_s < strike - 1))
+        def _():
+            wait_for(buf.at[planes + 1, pl.ds(1, NY)], recv.at[1])
+
+    def forward(step, bias_sum):
+        x = side(step)
+        got(field, fr, x)
+        for y, value in enumerate(outer_sums(field, wf_out, x)):
             pre = value + partial[x, y]
             sig = jax.nn.sigmoid(pre)
             rise = pre * sig
-            turned_out[pl.ds(x * CH * NY + y, CH, NY), :] = rise
-            upstream = work[pl.ds(y, CH, NY), :]
-            dpre = (upstream * (sig + rise * (1.0 - sig))).astype(BF16)
+            turned_out[pl.ds(x * (CH * NY) + y, CH, NY), :] = rise
+            slope = sig + rise * (1.0 - sig)
+            dpre = (upstream[x, y].astype(F32) * slope).astype(BF16)
             dgrad[x + 1, y + 1] = dpre
             wide = dpre.astype(F32)
             bias_sum = bias_sum + wide
@@ -282,21 +306,17 @@
             dshift[x, y, 0:CH] = before.astype(BF16)
             dshift[x, y, CH : 2 * CH] = dpre
             dshift[x, y, 2 * CH : 3 * CH] = after.astype(BF16)
+        return bias_sum
+
+    bias_sum = lax.fori_loop(0, planes, forward, jnp.zeros((CH, NZ), F32))
 
     send_halo(dgrad, ds, dr)
-    total = None
-    for x in range(planes):
-        left = jnp.concatenate(
-            [
-                jnp.concatenate([field[x + a, y + b] for y in range(NY)], axis=1)
-                for a in range(3)
-                for b in range(3)
-            ],
-            axis=0,
-        )
-        right = jnp.concatenate([dshift[x, y] for y in range(NY)], axis=1)
-        part = lax.dot_general(left, right, (((1,), (1,)), ((), ())), preferred_element_type=F32)
-        total = part if total is None else total + part
+    left = rows_of(field, (0, 1, 2, 3))
+    right = jnp.concatenate(
+        [jnp.concatenate([dshift[x, y] for y in range(NY)], axis=1) for x in range(2)], axis=0
+    )
+    both = lax.dot_general(left, right, (((1,), (1,)), ((), ())), preferred_element_type=F32)
+    total = both[: 9 * CH, : 3 * CH] + both[3 * CH :, 3 * CH :]
     total = jnp.concatenate([total, jnp.zeros((9 * CH, CH), F32)], axis=1)
     total = jnp.concatenate([total, jnp.zeros((3 * CH, 4 * CH), F32)], axis=0)
     total = jnp.concatenate(
@@ -344,15 +364,13 @@
 
     pack(act_out)
     turned = jnp.concatenate([whole[:, :128].T, whole[:, 128:].T], axis=0)
-    for c in range(3):
-        back = []
-        for ab in range(9):
-            t = 26 - (3 * ab + c)
-            back.append(turned[(t % 8) * CH : (t % 8 + 1) * CH, (t // 8) * CH : (t // 8 + 1) * CH])
-        wb[pl.ds(c * CH, CH), :] = jnp.concatenate(back, axis=1).astype(BF16)
-    for x in range(planes):
-        for y, value in enumerate(stencil(dgrad, wb, x, sides[x])):
-            partial[x, y] = value
+
+    def backward_tap(c, ab):
+        t = 26 - (3 * ab + c)
+        return turned[(t % 8) * CH : (t % 8 + 1) * CH, (t // 8) * CH : (t // 8 + 1) * CH]
+
+    lay_out(backward_tap, wb_in, wb_out)
+    inner_sums(dgrad, wb_in, partial, None)
 
     own.wait()
     wait_for(recv1.at[pl.ds(0, members - 1)], r1)
@@ -377,10 +395,14 @@
 
     lax.fori_loop(1, strike, spread_sum, 0)
 
-    for x in range(planes):
-        (got_below if x == 0 else got_above)(dgrad, dr)
-        for y, value in enumerate(stencil(dgrad, wb, x, edges[x])):
-            turned_out[pl.ds(x * CH * NY + y, CH, NY), :] = value + partial[x, y]
+    def backward(step, carry):
+        x = side(step)
+        got(dgrad, dr, x)
+        for y, value in enumerate(outer_sums(dgrad, wb_out, x)):
+            turned_out[pl.ds(x * (CH * NY) + y, CH, NY), :] = value + partial[x, y]
+        return carry
+
+    lax.fori_loop(0, planes, backward, 0)
     pack(gin_out)
 
     wait_for(recv2.at[pl.ds(0, strike - 1)], r2)
@@ -443,14 +465,17 @@
         ((rows, 27 * CH), BF16),
         ((1, rows), BF16),
         ((CH * NY, NZ), F32),
+        ((planes, NY, CH, NZ), BF16),
         ((planes * CH * NY, NZ), F32),
         ((planes, NY, CH, NZ), F32),
         ((planes + 2, NY + 2, CH, NZ), BF16),
         ((planes + 2, NY + 2, CH, NZ), BF16),
         ((planes, NY, 3 * CH, NZ), BF16),
         ((rows * 4, 256), BF16),
-        ((3 * CH, 9 * CH), BF16),
-        ((3 * CH, 9 * CH), BF16),
+        ((6 * CH, 6 * CH), BF16),
+        ((2, 3 * CH, 3 * CH), BF16),
+        ((6 * CH, 6 * CH), BF16),
+        ((2, 3 * CH, 3 * CH), BF16),
         ((CH, NZ), F32),
         ((real, rows * 4, 256), BF16),
         ((CH * 8, 128), F32),

time: 33.2 us -> 32.1 us (0.967)
  Pallas kernels: 32.4 us -> 31.3 us
    pallas_call x1, Pallas kernels: 31.4 us -> 30.3 us  [local(): pl.pallas_call(functools.partial(kernel, real, xl, zs, co, planes, factor...]
where the time goes in v5:
time: 32.1 us; the launch traced here: 31.9 us
  Pallas kernels  31.3 us (98%)
  between operations  0.64 us (2%)
    pallas_call x1, Pallas kernels, local(): pl.pallas_call(functools.partial(kernel, real, xl, zs, co, planes, factor...  30.3 us
    pallas_call x1, Pallas kernels, local(): pl.pallas_call(functools.partial(place, rows), out_shape=(block, block, j...  1.01 us

profile of v5, /device:TPU:1, one launch (start us, length us, event | category | flops | bytes accessed | tf_op | source)
XLA Modules:
  0.0 31.9 jit_solution(14318854958032854768)
XLA Ops:
  0.6 30.3 %shard_map.75 = (bf16[1,32,2,32,128]{4,3,2,1,0:T(8,128)(2,1)S(1)}, bf16[1,32,2,32,128]{4,3,2,1,0:T(8,128)(2,1)S(1)}, f32[32,128]{1,0:T(8,128)S(1)}) custom-call(bf16[1,32,2,32,128]{4,3,2,1,0:T(8,128)(2,1)} %grades.1, bf16[1,32,2,32,128]{4,3,2,1,0:T(8,128)(2,1)} %cot.1, bf16[4,864]{1,0:T(4,128)(2,1)} %weight.1, bf16[1,4]{1,0:T(2,128)(2,1)} %bitcast.2), custom_call_target="tpu_custom_call" | custom-call | tf_op jit(solution)/shard_map/pallas_call | solution.py:487
  30.9 1.0 %shard_map.76 = (bf16[1,32,2,32,128]{4,3,2,1,0:T(8,128)(2,1)}, bf16[1,32,2,32,128]{4,3,2,1,0:T(8,128)(2,1)}, f32[4,864]{1,0:T(4,128)}, f32[1,4]{1,0:T(1,128)}) custom-call(bf16[1,32,2,32,128]{4,3,2,1,0:T(8,128)(2,1)S(1)} %get-tuple-element.11.act, bf16[1,32,2,32,128]{4,3,2,1,0:T(8,128)(2,1)S(1)} %get-tuple-element.12.gin, f32[32,128]{1,0:T(8,128)S(1)} %get-tuple-element.13.total), custom_call_target="tpu_custom_call" | custom-call | tf_op jit(solution)/shard_map/pallas_call | solution.py:504
